TPU v7x, 512 devices: a whole 4x4x16 slice. The times are simulated.
512 devices in a mesh: dp: 64 (over x, z), tensor: 8 (over y, core).
Axes of the slice: x: 4, y: 4, z: 16, core: 2. Of those that a mesh axis runs over, the one named last changes fastest.
Arguments:
- hidden: bfloat16 [8192, 5120], P('dp', 'tensor'), may hold values from -6 to 6
- queries: bfloat16 [8192, 8192], P('dp', 'tensor'), may hold values from -21 to 21
- out_grad: bfloat16 [8192, 8192], P('dp', 'tensor'), may hold values from -16 to 16
- w_key: bfloat16 [5120, 1024], P(None, 'tensor'), may hold values from -0.078125 to 0.078125
- w_value: bfloat16 [5120, 1024], P(None, 'tensor'), may hold values from -0.078125 to 0.078125
- prompt_kv: bfloat16 [64, 2, 1024, 1024], P('dp', None, None, 'tensor'), may hold values from -6 to 6
- block_dest: int32 [64], replicated, may hold values from 0 to 63, as said below
- resp_len: int32 [64], replicated, may hold values from 1 to 128, as said below
Outputs:
- grad_query: bfloat16 [8192, 8192], P('dp', 'tensor')
- grad_hidden: bfloat16 [8192, 5120], P('dp', 'tensor')
- grad_prompt_kv: bfloat16 [64, 2, 1024, 1024], P('dp', None, None, 'tensor')
Inputs may be any that keep to these rules, and one draw needn't show every extreme that they name: block_dest[b] // 4 == b // 4; no shard is the destination of more than 3 blocks, and in every draw some shard is the destination of exactly 3. `resp_len`: some block is full in every draw.
All inputs are finite; a program needn't handle non-finite values.
Results may differ from a plain program's by a relative error of at most 0.019.
Values may be sent and summed in bfloat16 or wider, within the bound.
A program may use at most 64 MiB of HBM per device.

v0:
```python
import math

import jax
import jax.numpy as jnp
from jax import lax
from jax.sharding import PartitionSpec as P

HD = 128
GROUP = 4
CAP = 3


big_negative = -1e30


def from_behind(block, axis, distance):
    devices = range(lax.axis_size(axis))
    route = [(i - distance, i) for i in devices if i - distance in devices]
    return lax.ppermute(block, axis, route)


def block_grads(query_rows, resp_keys, resp_values, upstream_rows, prompt_pair, length):
    row_count = query_rows.shape[0]
    kv_cols = resp_keys.shape[1]
    group_size = query_rows.shape[1] // kv_cols
    group_cols = group_size * HD
    score_scale = 1.0 / math.sqrt(HD)
    prompt_len = prompt_pair.shape[1]
    all_keys = jnp.concatenate([prompt_pair[0], resp_keys], axis=0)
    all_values = jnp.concatenate([prompt_pair[1], resp_values], axis=0)
    key_count = all_keys.shape[0]
    row_pos = lax.broadcasted_iota(jnp.int32, (row_count, key_count), 0)
    col_pos = lax.broadcasted_iota(jnp.int32, (row_count, key_count), 1) - prompt_len
    visible = (col_pos < 0) | (col_pos <= row_pos) & (col_pos < length)
    live_rows = lax.broadcasted_iota(jnp.int32, (row_count, 1, 1), 0) < length
    query_head = query_rows.reshape(row_count, group_size, HD)
    upstream_head = upstream_rows.reshape(row_count, group_size, HD)
    upstream_head = jnp.where(live_rows, upstream_head, jnp.zeros((), jnp.bfloat16))
    scores = (
        jnp.einsum("igd,jd->gij", query_head, all_keys, preferred_element_type=jnp.float32)
        * score_scale
    )
    scores = jnp.where(visible[None], scores, big_negative)
    row_peak = jnp.max(scores, axis=2, keepdims=True)
    exponent = jnp.exp(scores - row_peak)
    softmax_out = exponent / jnp.sum(exponent, axis=2, keepdims=True)
    weights = softmax_out.astype(jnp.bfloat16)
    attended = jnp.einsum("gij,jd->igd", weights, all_values, preferred_element_type=jnp.float32)
    row_dot = jnp.sum(upstream_head.astype(jnp.float32) * attended, axis=2)
    prob_grad = jnp.einsum(
        "igd,jd->gij", upstream_head, all_values, preferred_element_type=jnp.float32
    )
    score_grad = (softmax_out * (prob_grad - row_dot.T[:, :, None])).astype(jnp.bfloat16)
    query_grad = (
        jnp.einsum("gij,jd->igd", score_grad, all_keys, preferred_element_type=jnp.float32)
        * score_scale
    )
    query_grads = query_grad.astype(jnp.bfloat16).reshape(row_count, group_cols)
    key_grads = (
        jnp.einsum("gij,igd->jd", score_grad, query_head, preferred_element_type=jnp.float32)
        * score_scale
    )
    value_grads = jnp.einsum(
        "gij,igd->jd", weights, upstream_head, preferred_element_type=jnp.float32
    )
    prompt_grad = jnp.stack([key_grads[:prompt_len], value_grads[:prompt_len]]).astype(jnp.bfloat16)
    return (
        query_grads,
        key_grads[prompt_len:].astype(jnp.bfloat16),
        value_grads[prompt_len:].astype(jnp.bfloat16),
        prompt_grad,
    )


def holder_slots(stacked, is_valid, lengths, prompt_pair, query_cols, kv_cols):
    slot_total = stacked.shape[0]
    slot_ids = jnp.arange(slot_total, dtype=jnp.int32)
    slot_order = jnp.argsort(jnp.where(is_valid, slot_ids, slot_ids + slot_total))[:CAP]
    chosen_valid = is_valid[slot_order]
    prompt_sum = jnp.zeros(prompt_pair.shape, jnp.float32)
    results = []
    for slot_number in range(CAP):
        block_data = stacked[slot_order[slot_number]]
        grad_query, grad_key, grad_value, prompt_grad = block_grads(
            block_data[:, :query_cols],
            block_data[:, query_cols : query_cols + kv_cols],
            block_data[:, query_cols + kv_cols : query_cols + 2 * kv_cols],
            block_data[:, query_cols + 2 * kv_cols :],
            prompt_pair,
            lengths[slot_order[slot_number]],
        )
        prompt_sum = prompt_sum + jnp.where(
            chosen_valid[slot_number], prompt_grad.astype(jnp.float32), 0.0
        )
        results.append(jnp.concatenate([grad_query, grad_key, grad_value], axis=1))
    outgoing_list = []
    for position in range(slot_total):
        outgoing = jnp.zeros_like(results[0])
        for slot_number in range(CAP):
            taken = (slot_order[slot_number] == position) & chosen_valid[slot_number]
            outgoing = jnp.where(taken, results[slot_number], outgoing)
        outgoing_list.append(outgoing)
    return (prompt_sum.astype(jnp.bfloat16)[None], outgoing_list)


def local(hidden, queries, out_grad, w_key, w_value, prompt_kv, block_dest, resp_len):
    own_index = lax.axis_index("dp")
    nblocks = block_dest.shape[0]
    full_hidden = lax.all_gather(hidden, "tensor", axis=1, tiled=True)
    resp_keys = jnp.dot(full_hidden, w_key, preferred_element_type=jnp.float32).astype(jnp.bfloat16)
    resp_values = jnp.dot(full_hidden, w_value, preferred_element_type=jnp.float32).astype(
        jnp.bfloat16
    )
    own_offset = block_dest[own_index] - own_index
    offsets = list(range(1 - GROUP, GROUP))
    query_cols = queries.shape[1]
    kv_cols = resp_keys.shape[1]
    packed = jnp.concatenate([queries, resp_keys, resp_values, out_grad], axis=1)
    arrived = []
    for offset in offsets:
        if offset == 0:
            arrived.append(packed)
        else:
            arrived.append(from_behind(packed, "dp", offset))
    stacked = jnp.stack(arrived)
    sources = own_index - jnp.asarray(offsets, jnp.int32)
    inside = (sources >= 0) & (sources < nblocks)
    safe_sources = jnp.clip(sources, 0, nblocks - 1)
    is_valid = inside & (block_dest[safe_sources] == own_index)
    lengths = resp_len[safe_sources]
    grad_prompt, outgoing_list = holder_slots(
        stacked, is_valid, lengths, prompt_kv[0], query_cols, kv_cols
    )
    own_result = jnp.zeros_like(outgoing_list[0])
    for position, offset in enumerate(offsets):
        if offset == 0:
            returned = outgoing_list[position]
        else:
            returned = from_behind(outgoing_list[position], "dp", -offset)
        own_result = jnp.where(own_offset == offset, returned, own_result)
    grad_query = own_result[:, :query_cols]
    grad_key = own_result[:, query_cols : query_cols + kv_cols]
    grad_value = own_result[:, query_cols + kv_cols :]
    partial_value = jnp.einsum("ic,dc->id", grad_key, w_key, preferred_element_type=jnp.float32)
    partial_value = partial_value + jnp.einsum(
        "ic,dc->id", grad_value, w_value, preferred_element_type=jnp.float32
    )
    summed = lax.psum(partial_value.astype(jnp.bfloat16), "tensor").astype(jnp.float32)
    share_cols = hidden.shape[1]
    grad_hidden = lax.dynamic_slice_in_dim(
        summed, lax.axis_index("tensor") * share_cols, share_cols, 1
    )
    return (grad_query, grad_hidden.astype(jnp.bfloat16), grad_prompt)


def solution(mesh):
    return jax.shard_map(
        local,
        mesh=mesh,
        in_specs=(
            P("dp", "tensor"),
            P("dp", "tensor"),
            P("dp", "tensor"),
            P(None, "tensor"),
            P(None, "tensor"),
            P("dp", None, None, "tensor"),
            P(),
            P(),
        ),
        out_specs=(P("dp", "tensor"), P("dp", "tensor"), P("dp", None, None, "tensor")),
        check_vma=False,
    )
```

profile of v0, /device:TPU:1, one launch (start us, length us, event | category | flops | bytes accessed | tf_op | source)
XLA Modules:
  0.0 378.7 jit_solution(8415990026997457769)
XLA Ops:
  8.7 1.4 gather_fusion
  25.7 22.0 %all-gather.2.cloned.1.call-done = bf16[128,5120]{1,0:T(8,128)(2,1)} async-done(((bf16[128,640]{1,0:T(8,128)(2,1)}), bf16[128,5120]{1,0:T(8,128)(2,1)}) %all-gather.2.cloned.1.call-update) | async-done | bytes 1310736 | tf_op jit(solution)/shard_map/all_gather | solution.py:109
  47.6 1.9 convolution_convert_fusion
  49.7 1.9 convolution_convert_fusion.1
  51.8 1.8 pad_maximum_fusion
  83.3 2.3 fusion.46
  88.2 4.0 %collective-permute-start.3 = (bf16[128,2304]{1,0:T(8,128)(2,1)}, bf16[128,2304]{1,0:T(8,128)(2,1)S(1)}, u32[]{:S(2)}, u32[]{:S(2)}) collective-permute-start(bf16[128,2304]{1,0:T(8,128)(2,1)} %pad_maximum_fusion), channel_id=1, source_target_pairs={{0,8},{8,16},{16,24},{24,32},{32,40},{40,48},{48,56},{56,64},{64,7... | collective-permute-start | bytes 1769480 | tf_op jit(solution)/shard_map/ppermute | solution.py:19
  92.2 5.2 %collective-permute-start.4 = (bf16[128,2304]{1,0:T(8,128)(2,1)}, bf16[128,2304]{1,0:T(8,128)(2,1)S(1)}, u32[]{:S(2)}, u32[]{:S(2)}) collective-permute-start(bf16[128,2304]{1,0:T(8,128)(2,1)} %pad_maximum_fusion), channel_id=1, source_target_pairs={{0,16},{8,24},{16,32},{24,40},{32,48},{40,56},{48,64},{56,72},{64,... | collective-permute-start | bytes 1769480 | tf_op jit(solution)/shard_map/ppermute | solution.py:19
  97.5 6.8 %collective-permute-start.5 = (bf16[128,2304]{1,0:T(8,128)(2,1)}, bf16[128,2304]{1,0:T(8,128)(2,1)S(1)}, u32[]{:S(2)}, u32[]{:S(2)}) collective-permute-start(bf16[128,2304]{1,0:T(8,128)(2,1)} %pad_maximum_fusion), channel_id=1, source_target_pairs={{0,24},{8,32},{16,40},{24,48},{32,56},{40,64},{48,72},{56,80},{64,... | collective-permute-start | bytes 1769480 | tf_op jit(solution)/shard_map/ppermute | solution.py:19
  105.4 18.8 %collective-permute-done.1 = bf16[128,2304]{1,0:T(8,128)(2,1)S(1)} collective-permute-done((bf16[128,2304]{1,0:T(8,128)(2,1)}, bf16[128,2304]{1,0:T(8,128)(2,1)S(1)}, u32[]{:S(2)}, u32[]{:S(2)}) %collective-permute-start.1) | collective-permute-done | bytes 589856 | tf_op jit(solution)/shard_map/ppermute | solution.py:19
  124.5 7.5 %collective-permute-done.5 = bf16[128,2304]{1,0:T(8,128)(2,1)S(1)} collective-permute-done((bf16[128,2304]{1,0:T(8,128)(2,1)}, bf16[128,2304]{1,0:T(8,128)(2,1)S(1)}, u32[]{:S(2)}, u32[]{:S(2)}) %collective-permute-start.5) | collective-permute-done | bytes 589856 | tf_op jit(solution)/shard_map/ppermute | solution.py:19
  136.0 4.8 %exponential_reduce_fusion = (f32[8,128]{1,0:T(8,128)S(1)}, f32[8,128,1152]{1,2,0:T(8,128)}) fusion(pred[128,1152]{0,1:T(8,128)(4,1)} %get-tuple-element.31, bf16[128,8,128]{0,2,1:T(8,128)(2,1)} %bitcast.243, bf16[128,128]{1,0:T(8,128)(2,1)S(1)} %get-tuple-element.25, bf16[1024,128]{1,0:T(8,128)(2,1)S(1)} %get-tuple-element.29), kind=kOutput, calls=%fused_computation.30 | convolution fusion | flops 307299456 | bytes 5427200 | tf_op jit(solution)/shard_map/sub | solution.py:45
  140.7 3.1 fusion.33
  143.9 1.6 fusion.24
  147.2 1.6 fusion.23
  153.0 4.8 %exponential_reduce_fusion.1 = (f32[8,128]{1,0:T(8,128)S(1)}, f32[8,128,1152]{1,2,0:T(8,128)}) fusion(pred[128,1152]{0,1:T(8,128)(4,1)} %get-tuple-element.32, bf16[128,8,128]{0,2,1:T(8,128)(2,1)} %bitcast.245, bf16[128,128]{1,0:T(8,128)(2,1)S(1)} %get-tuple-element.52, bf16[1024,128]{1,0:T(8,128)(2,1)S(1)} %get-tuple-element.29), kind=kOutput, calls=%fused_computation.32 | convolution fusion | flops 307299456 | bytes 5427200 | tf_op jit(solution)/shard_map/sub | solution.py:45
  157.8 3.1 fusion.32
  160.9 1.6 fusion.22
  164.2 1.6 fusion.21
  169.0 5.0 %exponential_reduce_fusion.2 = (f32[8,128]{1,0:T(8,128)S(1)}, f32[8,128,1152]{1,2,0:T(8,128)}) fusion(pred[128,1152]{0,1:T(8,128)(4,1)} %get-tuple-element.30, bf16[128,8,128]{0,2,1:T(8,128)(2,1)} %bitcast.241, bf16[128,128]{1,0:T(8,128)(2,1)S(1)} %get-tuple-element.17, bf16[1024,128]{1,0:T(8,128)(2,1)S(1)} %get-tuple-element.29), kind=kOutput, calls=%fused_computation.34 | convolution fusion | flops 307299456 | bytes 5427200 | tf_op jit(solution)/shard_map/sub | solution.py:45
  174.0 3.1 fusion.31
  177.2 1.6 fusion.20
  180.5 1.6 fusion.19
  191.7 1.4 collective-permute-start.7
  194.8 38.6 %collective-permute-start.9 = (bf16[128,1280]{1,0:T(8,128)(2,1)S(1)}, bf16[128,1280]{1,0:T(8,128)(2,1)S(1)}, u32[]{:S(2)}, u32[]{:S(2)}) collective-permute-start(bf16[128,1280]{1,0:T(8,128)(2,1)S(1)} %select_select_fusion.3), channel_id=1, source_target_pairs={{0,8},{8,16},{16,24},{24,32},{32,40},{40,48},{48,56},{56,64},{64,7... | collective-permute-start | bytes 983048 | tf_op jit(solution)/shard_map/ppermute | solution.py:19
  233.6 7.2 %collective-permute-start.10 = (bf16[128,1280]{1,0:T(8,128)(2,1)S(1)}, bf16[128,1280]{1,0:T(8,128)(2,1)S(1)}, u32[]{:S(2)}, u32[]{:S(2)}) collective-permute-start(bf16[128,1280]{1,0:T(8,128)(2,1)S(1)} %select_select_fusion.2), channel_id=1, source_target_pairs={{0,16},{8,24},{16,32},{24,40},{32,48},{40,56},{48,64},{56,72},{64,... | collective-permute-start | bytes 983048 | tf_op jit(solution)/shard_map/ppermute | solution.py:19
  241.0 19.3 %collective-permute-start.11 = (bf16[128,1280]{1,0:T(8,128)(2,1)S(1)}, bf16[128,1280]{1,0:T(8,128)(2,1)S(1)}, u32[]{:S(2)}, u32[]{:S(2)}) collective-permute-start(bf16[128,1280]{1,0:T(8,128)(2,1)S(1)} %select_select_fusion.1), channel_id=1, source_target_pairs={{0,24},{8,32},{16,40},{24,48},{32,56},{40,64},{48,72},{56,80},{64,... | collective-permute-start | bytes 983048 | tf_op jit(solution)/shard_map/ppermute | solution.py:19
  261.7 4.3 %collective-permute-done.11 = bf16[128,1280]{1,0:T(8,128)(2,1)S(1)} collective-permute-done((bf16[128,1280]{1,0:T(8,128)(2,1)S(1)}, bf16[128,1280]{1,0:T(8,128)(2,1)S(1)}, u32[]{:S(2)}, u32[]{:S(2)}) %collective-permute-start.11) | collective-permute-done | bytes 327712 | tf_op jit(solution)/shard_map/ppermute | solution.py:19
  267.2 1.6 fusion.3
  271.0 2.1 add_convert_fusion
  274.8 95.5 %all-reduce.2.cloned.1.call-done = bf16[128,5120]{1,0:T(8,128)(2,1)} async-done(((bf16[128,5120]{1,0:T(8,128)(2,1)}), bf16[128,5120]{1,0:T(8,128)(2,1)}) %all-reduce.2.cloned.1.call-update) | async-done | bytes 1310736 | tf_op jit(solution)/shard_map/psum | solution.py:148
  370.3 1.6 convert_convert_fusion
  (165 shorter events, 52.1 us)
Async XLA Ops:
  7.2 40.5 %copy-start = (bf16[5120,128]{1,0:T(8,128)(2,1)S(1)}, bf16[5120,128]{1,0:T(8,128)(2,1)}, u32[]{:S(2)}) copy-start(bf16[5120,128]{1,0:T(8,128)(2,1)} %param.13) | copy-start | bytes 3932164
  7.2 40.4 %all-gather.2.cloned.1.call-start = ((), (), s32[]{:S(2)}) async-start(), calls=%async_computation | async-start | bytes 1474560 | tf_op jit(solution)/shard_map/all_gather | solution.py:109
  7.9 362.4 %all-reduce.2.cloned.1.call-start = ((), (), s32[]{:S(2)}) async-start(), calls=%async_computation.1 | async-start | bytes 2621440 | tf_op jit(solution)/shard_map/psum | solution.py:148
  8.6 41.1 %copy-start.2 = (bf16[5120,128]{1,0:T(8,128)(2,1)S(1)}, bf16[5120,128]{1,0:T(8,128)(2,1)}, u32[]{:S(2)}) copy-start(bf16[5120,128]{1,0:T(8,128)(2,1)} %param.12) | copy-start | bytes 3932164
  25.7 26.1 %copy-start.13 = (bf16[128,1024]{1,0:T(8,128)(2,1)S(1)}, bf16[128,1024]{1,0:T(8,128)(2,1)}, u32[]{:S(2)}) copy-start(bf16[128,1024]{1,0:T(8,128)(2,1)} %param.11) | copy-start | bytes 786436
  49.6 19.6 %copy-start.1 = (s32[64]{0:T(128)S(1)}, s32[64]{0:T(128)}, u32[]{:S(2)}) copy-start(s32[64]{0:T(128)} %param.15) | copy-start | bytes 772
  53.6 43.9 %collective-permute-start = (bf16[128,2304]{1,0:T(8,128)(2,1)}, bf16[128,2304]{1,0:T(8,128)(2,1)}, u32[]{:S(2)}, u32[]{:S(2)}) collective-permute-start(bf16[128,2304]{1,0:T(8,128)(2,1)} %pad_maximum_fusion), channel_id=1, source_target_pairs={{24,0},{32,8},{40,16},{48,24},{56,32},{64,40},{72,48},{80,56},{88,... | collective-permute-start | bytes 1769480 | tf_op jit(solution)/shard_map/ppermute | solution.py:19
  83.3 41.0 %copy-start.14 = (bf16[128,1024]{1,0:T(8,128)(2,1)S(1)}, bf16[128,1024]{1,0:T(8,128)(2,1)}, u32[]{:S(2)}) copy-start(bf16[128,1024]{1,0:T(8,128)(2,1)} %param.10) | copy-start | bytes 786436
  85.6 38.6 %collective-permute-start.1 = (bf16[128,2304]{1,0:T(8,128)(2,1)}, bf16[128,2304]{1,0:T(8,128)(2,1)S(1)}, u32[]{:S(2)}, u32[]{:S(2)}) collective-permute-start(bf16[128,2304]{1,0:T(8,128)(2,1)} %pad_maximum_fusion), channel_id=1, source_target_pairs={{16,0},{24,8},{32,16},{40,24},{48,32},{56,40},{64,48},{72,56},{80,... | collective-permute-start | bytes 1769480 | tf_op jit(solution)/shard_map/ppermute | solution.py:19
  86.9 37.4 %collective-permute-start.2 = (bf16[128,2304]{1,0:T(8,128)(2,1)}, bf16[128,2304]{1,0:T(8,128)(2,1)S(1)}, u32[]{:S(2)}, u32[]{:S(2)}) collective-permute-start(bf16[128,2304]{1,0:T(8,128)(2,1)} %pad_maximum_fusion), channel_id=1, source_target_pairs={{8,0},{16,8},{24,16},{32,24},{40,32},{48,40},{56,48},{64,56},{72,6... | collective-permute-start | bytes 1769480 | tf_op jit(solution)/shard_map/ppermute | solution.py:19
  88.2 36.2 %collective-permute-start.3 = (bf16[128,2304]{1,0:T(8,128)(2,1)}, bf16[128,2304]{1,0:T(8,128)(2,1)S(1)}, u32[]{:S(2)}, u32[]{:S(2)}) collective-permute-start(bf16[128,2304]{1,0:T(8,128)(2,1)} %pad_maximum_fusion), channel_id=1, source_target_pairs={{0,8},{8,16},{16,24},{24,32},{32,40},{40,48},{48,56},{56,64},{64,7... | collective-permute-start | bytes 1769480 | tf_op jit(solution)/shard_map/ppermute | solution.py:19
  92.2 32.2 %collective-permute-start.4 = (bf16[128,2304]{1,0:T(8,128)(2,1)}, bf16[128,2304]{1,0:T(8,128)(2,1)S(1)}, u32[]{:S(2)}, u32[]{:S(2)}) collective-permute-start(bf16[128,2304]{1,0:T(8,128)(2,1)} %pad_maximum_fusion), channel_id=1, source_target_pairs={{0,16},{8,24},{16,32},{24,40},{32,48},{40,56},{48,64},{56,72},{64,... | collective-permute-start | bytes 1769480 | tf_op jit(solution)/shard_map/ppermute | solution.py:19
  97.5 34.5 %collective-permute-start.5 = (bf16[128,2304]{1,0:T(8,128)(2,1)}, bf16[128,2304]{1,0:T(8,128)(2,1)S(1)}, u32[]{:S(2)}, u32[]{:S(2)}) collective-permute-start(bf16[128,2304]{1,0:T(8,128)(2,1)} %pad_maximum_fusion), channel_id=1, source_target_pairs={{0,24},{8,32},{16,40},{24,48},{32,56},{40,64},{48,72},{56,80},{64,... | collective-permute-start | bytes 1769480 | tf_op jit(solution)/shard_map/ppermute | solution.py:19
  140.7 5.3 %slice-start = ((s8[4718592]{0:T(1024)(128)(4,1)}), s8[4194304]{0:T(1024)(128)(4,1)S(1)}, s32[]{:S(2)}) async-start(s8[4718592]{0:T(1024)(128)(4,1)} %bitcast.223), calls=%async_computation.2 | async-start | bytes 8388608
  157.8 5.3 %slice-start.4 = ((s8[4718592]{0:T(1024)(128)(4,1)}), s8[4194304]{0:T(1024)(128)(4,1)S(1)}, s32[]{:S(2)}) async-start(s8[4718592]{0:T(1024)(128)(4,1)} %bitcast.227), calls=%async_computation.6 | async-start | bytes 8388608
  174.0 5.3 %slice-start.2 = ((s8[4718592]{0:T(1024)(128)(4,1)}), s8[4194304]{0:T(1024)(128)(4,1)S(1)}, s32[]{:S(2)}) async-start(s8[4718592]{0:T(1024)(128)(4,1)} %bitcast.225), calls=%async_computation.4 | async-start | bytes 8388608
  182.1 2.3 copy-start.10
  182.1 2.4 slice-start.10
  182.1 2.6 slice-start.6
  182.1 3.8 slice-start.7
  182.1 4.5 %slice-start.9 = ((bf16[1152,128]{0,1:T(8,128)(2,1)}), bf16[128,128]{0,1:T(8,128)(2,1)S(1)}, s32[]{:S(2)}) async-start(bf16[1152,128]{0,1:T(8,128)(2,1)} %fusion.19), calls=%async_computation.11 | async-start | bytes 65536 | tf_op jit(solution)/shard_map/slice | solution.py:69
  188.4 4.7 %copy-start.5 = (bf16[128,128]{1,0:T(8,128)(2,1)S(1)}, bf16[128,128]{1,0:T(8,128)(2,1)}, u32[]{:S(2)}) copy-start(bf16[128,128]{1,0:T(8,128)(2,1)} %copy.67) | copy-start | bytes 98308
  188.4 4.7 %copy-start.6 = (bf16[128,128]{1,0:T(8,128)(2,1)S(1)}, bf16[128,128]{1,0:T(8,128)(2,1)}, u32[]{:S(2)}) copy-start(bf16[128,128]{1,0:T(8,128)(2,1)} %copy.66) | copy-start | bytes 98308
  189.4 51.5 %collective-permute-start.6 = (bf16[128,1280]{1,0:T(8,128)(2,1)S(1)}, bf16[128,1280]{1,0:T(8,128)(2,1)S(1)}, u32[]{:S(2)}, u32[]{:S(2)}) collective-permute-start(bf16[128,1280]{1,0:T(8,128)(2,1)S(1)} %select_select_fusion.6), channel_id=1, source_target_pairs={{24,0},{32,8},{40,16},{48,24},{56,32},{64,40},{72,48},{80,56},{88,... | collective-permute-start | bytes 983048 | tf_op jit(solution)/shard_map/ppermute | solution.py:19
  191.7 68.5 %copy-start.17 = (bf16[1152,128]{0,1:T(8,128)(2,1)S(1)}, bf16[1152,128]{0,1:T(8,128)(2,1)}, u32[]{:S(2)}) copy-start(bf16[1152,128]{0,1:T(8,128)(2,1)} %fusion.23) | copy-start | bytes 884740
  191.7 69.3 %copy-start.18 = (bf16[1152,128]{0,1:T(8,128)(2,1)S(1)}, bf16[1152,128]{0,1:T(8,128)(2,1)}, u32[]{:S(2)}) copy-start(bf16[1152,128]{0,1:T(8,128)(2,1)} %fusion.22) | copy-start | bytes 884740
  191.7 70.0 %collective-permute-start.7 = (bf16[128,1280]{1,0:T(8,128)(2,1)S(1)}, bf16[128,1280]{1,0:T(8,128)(2,1)S(1)}, u32[]{:S(2)}, u32[]{:S(2)}) collective-permute-start(bf16[128,1280]{1,0:T(8,128)(2,1)S(1)} %select_select_fusion.5), channel_id=1, source_target_pairs={{16,0},{24,8},{32,16},{40,24},{48,32},{56,40},{64,48},{72,56},{80,... | collective-permute-start | bytes 983048 | tf_op jit(solution)/shard_map/ppermute | solution.py:19
  193.4 68.4 %collective-permute-start.8 = (bf16[128,1280]{1,0:T(8,128)(2,1)S(1)}, bf16[128,1280]{1,0:T(8,128)(2,1)S(1)}, u32[]{:S(2)}, u32[]{:S(2)}) collective-permute-start(bf16[128,1280]{1,0:T(8,128)(2,1)S(1)} %select_select_fusion.4), channel_id=1, source_target_pairs={{8,0},{16,8},{24,16},{32,24},{40,32},{48,40},{56,48},{64,56},{72,6... | collective-permute-start | bytes 983048 | tf_op jit(solution)/shard_map/ppermute | solution.py:19
  194.8 66.9 %collective-permute-start.9 = (bf16[128,1280]{1,0:T(8,128)(2,1)S(1)}, bf16[128,1280]{1,0:T(8,128)(2,1)S(1)}, u32[]{:S(2)}, u32[]{:S(2)}) collective-permute-start(bf16[128,1280]{1,0:T(8,128)(2,1)S(1)} %select_select_fusion.3), channel_id=1, source_target_pairs={{0,8},{8,16},{16,24},{24,32},{32,40},{40,48},{48,56},{56,64},{64,7... | collective-permute-start | bytes 983048 | tf_op jit(solution)/shard_map/ppermute | solution.py:19
  233.6 28.1 %collective-permute-start.10 = (bf16[128,1280]{1,0:T(8,128)(2,1)S(1)}, bf16[128,1280]{1,0:T(8,128)(2,1)S(1)}, u32[]{:S(2)}, u32[]{:S(2)}) collective-permute-start(bf16[128,1280]{1,0:T(8,128)(2,1)S(1)} %select_select_fusion.2), channel_id=1, source_target_pairs={{0,16},{8,24},{16,32},{24,40},{32,48},{40,56},{48,64},{56,72},{64,... | collective-permute-start | bytes 983048 | tf_op jit(solution)/shard_map/ppermute | solution.py:19
  241.0 25.1 %collective-permute-start.11 = (bf16[128,1280]{1,0:T(8,128)(2,1)S(1)}, bf16[128,1280]{1,0:T(8,128)(2,1)S(1)}, u32[]{:S(2)}, u32[]{:S(2)}) collective-permute-start(bf16[128,1280]{1,0:T(8,128)(2,1)S(1)} %select_select_fusion.1), channel_id=1, source_target_pairs={{0,24},{8,32},{16,40},{24,48},{32,56},{40,64},{48,72},{56,80},{64,... | collective-permute-start | bytes 983048 | tf_op jit(solution)/shard_map/ppermute | solution.py:19
  268.9 5.2 %copy-start.8 = (bf16[128,1280]{1,0:T(8,128)(2,1)S(1)}, bf16[128,1280]{1,0:T(8,128)(2,1)}, u32[]{:S(2)}) copy-start(bf16[128,1280]{1,0:T(8,128)(2,1)} %copy-done.7) | copy-start | bytes 983044
  (17 other events, 27.8 us)
Sparse Core Ops, SparseCore 0:
  10.1 37.4 all-gather.1
  269.0 101.2 all-reduce.1
where the time goes:
time: 381 us; the launch traced here: 379 us
  waiting for transfers between devices  149 us (39%)
  starting transfers between devices  89 us (23%)
  between operations  47.9 us (13%)
  matrix products  38.9 us (10%)
  local copies, waits for them, and re-layouts  27.8 us (7%)
  other arithmetic  26.4 us (7%)
    psum x1, waiting for transfers between devices, local(): lax.psum(partial_value.astype(jnp.bfloat16), 'tensor').astype(jnp.float32)  95.5 us
    ppermute x12, starting transfers between devices, from_behind(): return lax.ppermute(block, axis, route)  89 us
    ppermute x12, waiting for transfers between devices, from_behind(): return lax.ppermute(block, axis, route)  30.7 us
    all_gather x1, waiting for transfers between devices, local(): full_hidden = lax.all_gather(hidden, 'tensor', axis=1, tiled=True)  22 us
    sub x3, matrix products, block_grads(): exponent = jnp.exp(scores - row_peak)  14.6 us
    convert_element_type x3, other arithmetic, block_grads(): weights = softmax_out.astype(jnp.bfloat16)  9.32 us
  transfers between devices with their start and end apart: 14, of which 5 were waited for; matrix products, arithmetic and copies ran while one was open for 7% of the time, Pallas kernels for 0%

commit v1 on v0

v1 whole, which is shorter than its diff:
```python
import math

import jax
import jax.numpy as jnp
from jax import lax
from jax.experimental import pallas as pl
from jax.experimental.pallas import tpu as pltpu
from jax.sharding import PartitionSpec as P

HD = 128
GROUP = 4
CHUNKS = 4
MESH = pl.DeviceIdType.MESH
BF16 = jnp.bfloat16
F32 = jnp.float32


def dot_nt(a, b):
    return lax.dot_general(a, b, (((1,), (1,)), ((), ())), preferred_element_type=F32)


def dot(a, b):
    return jnp.dot(a, b, preferred_element_type=F32)


def kernel(
    dest_ref, len_ref, hidden_ref, q_ref, u_ref, wk_ref, wv_ref, kv_ref,
    gq_out, gh_out, gp_out,
    own, fwd_a, fwd_b, fwd_c, fwd_relay, ret_own, ret_a, ret_b, ret_c, ret_relay, ret_sum,
    q_rows, u_rows, keys, scores, prob_grads, weights, score_grads,
    w, hid, sib_send, sib_recv, y_send, y_recv, gq_tile, gh_tile,
    fwd_s1, fwd_s2, fwd_ra, fwd_rb, fwd_rc, ret_s1, ret_s2, ret_ra, ret_rb, ret_rc,
    hid_ys, hid_yr, hid_ss, hid_sr, gh_ss, gh_sr, gh_ys, gh_yr,
    own_sem, q_sem, u_sem, w_sem, hid_sem, out_sem, gq_sem, gh_sem,
):
    rows = q_ref.shape[0]
    heads = q_ref.shape[1] // HD
    all_rows = heads * rows
    prompt_len = kv_ref.shape[1]
    key_count = prompt_len + rows
    chunk = prompt_len // CHUNKS
    total = 2 * CHUNKS
    shard_cols = hidden_ref.shape[1]
    scale = 1.0 / math.sqrt(HD)

    me = lax.axis_index("dp")
    r = lax.rem(me, GROUP)
    base = me - r
    mate = r + 1 - 2 * lax.rem(r, 2)
    opp = GROUP - 1 - r
    far = lax.rem(r + 2, GROUP)
    is_edge = (r == 0) | (r == GROUP - 1)
    is_middle = (r == 1) | (r == GROUP - 2)
    tensor = lax.axis_index("tensor")
    core = lax.rem(tensor, 2)
    y = tensor // 2
    sibling = tensor + 1 - 2 * core

    def y_peer(step):
        return lax.rem(y + step, 4) * 2 + core

    def along_z(src, dst, send, recv, place):
        return pltpu.make_async_remote_copy(
            src_ref=src, dst_ref=dst, send_sem=send, recv_sem=recv,
            device_id={"dp": base + place}, device_id_type=MESH,
        )

    def along_t(src, dst, send, recv, place):
        return pltpu.make_async_remote_copy(
            src_ref=src, dst_ref=dst, send_sem=send, recv_sem=recv,
            device_id={"tensor": place}, device_id_type=MESH,
        )

    def own_copy(c):
        return pltpu.make_async_copy(
            kv_ref.at[c // CHUNKS, pl.ds((c % CHUNKS) * chunk, chunk)], own.at[c], own_sem.at[c]
        )

    def head_copies(h):
        span = pl.ds(h * HD, HD)
        place = pl.ds(h * rows, rows)
        return (
            pltpu.make_async_copy(q_ref.at[:, span], q_rows.at[place], q_sem.at[h]),
            pltpu.make_async_copy(u_ref.at[:, span], u_rows.at[place], u_sem.at[h]),
        )

    w_copies = (
        pltpu.make_async_copy(wk_ref, w.at[:, :, pl.ds(0, HD)], w_sem.at[0]),
        pltpu.make_async_copy(wv_ref, w.at[:, :, pl.ds(HD, HD)], w_sem.at[1]),
    )
    hid_copy = pltpu.make_async_copy(hidden_ref, hid.at[0, 0], hid_sem)

    for h in range(heads):
        for copy in head_copies(h):
            copy.start()
    for c in range(total):
        own_copy(c).start()
    hid_copy.start()
    for copy in w_copies:
        copy.start()

    barrier = pltpu.get_barrier_semaphore()
    for step in range(1, GROUP):
        pl.semaphore_signal(
            barrier, inc=1, device_id={"dp": base + lax.rem(r + step, GROUP)}, device_id_type=MESH
        )
        pl.semaphore_signal(
            barrier, inc=1, device_id={"tensor": y_peer(step)}, device_id_type=MESH
        )
    pl.semaphore_signal(barrier, inc=1, device_id={"tensor": sibling}, device_id_type=MESH)
    pl.semaphore_wait(barrier, 2 * (GROUP - 1) + 1)

    def kv_part(c):
        return kv_ref.at[c // CHUNKS, pl.ds((c % CHUNKS) * chunk, chunk)]

    def fwd_near(c):
        return along_z(kv_part(c), fwd_a.at[c], fwd_s1.at[c], fwd_ra.at[c], mate)

    def fwd_far(c):
        return along_z(kv_part(c), fwd_c.at[c], fwd_s2.at[c], fwd_rc.at[c], far)

    def fwd_opp(c):
        return along_z(kv_part(c), fwd_b.at[c], fwd_s2.at[c], fwd_rb.at[c], opp)

    def fwd_relayed(c):
        return along_z(fwd_relay.at[c], fwd_a.at[c], fwd_s1.at[c], fwd_ra.at[c], mate)

    @pl.when(is_edge)
    def _():
        for c in range(total):
            fwd_far(c).start()
            fwd_near(c).start()

    @pl.when(is_middle)
    def _():
        for c in range(total):
            fwd_opp(c).start()

    def hid_to_y(step):
        return along_t(
            hidden_ref, hid.at[4 - step, 0], hid_ys.at[step], hid_yr.at[4 - step], y_peer(step)
        )

    def hid_from_y(step):
        return along_t(hidden_ref, hid.at[step, 0], hid_ys.at[step], hid_yr.at[step], y_peer(step))

    def hid_to_sibling(step):
        src = hidden_ref if step == 0 else hid.at[step, 0]
        return along_t(src, hid.at[step, 1], hid_ss.at[step], hid_sr.at[step], sibling)

    hid_to_sibling(0).start()
    for step in (2, 1, 3):
        hid_to_y(step).start()

    dest_of = [dest_ref[base + place] - base for place in range(GROUP)]
    my_dest = dest_ref[me] - base
    mate_dest = dest_ref[base + mate] - base
    opp_dest = dest_ref[base + opp] - base
    far_dest = dest_ref[base + far] - base
    length = len_ref[me]
    use_own = my_dest == r
    use_a = is_edge | (my_dest == mate)
    use_b = my_dest == opp

    def arrive(c):
        own_copy(c).wait()
        fwd_near(c).wait_recv()

        @pl.when(is_middle)
        def _():
            fwd_opp(c).wait_recv()
            along_z(kv_part(c), fwd_c.at[c], fwd_s2.at[c], fwd_rc.at[c], far).wait_recv()
            other = jnp.where(mate_dest == opp, fwd_b[c], fwd_c[c])
            fwd_relay[c] = jnp.where(mate_dest == r, own[c], other)
            fwd_relayed(c).start()

        other = jnp.where(use_b, fwd_b[c], fwd_c[c])
        return jnp.where(use_own, own[c], jnp.where(use_a, fwd_a[c], other))

    for h in range(heads):
        for copy in head_copies(h):
            copy.wait()

    def mask_upstream(h, carry):
        place = pl.ds(h * rows, rows)
        live = lax.broadcasted_iota(jnp.int32, (rows, HD), 0) < length
        u_rows[place] = jnp.where(live, u_rows[place].astype(F32), 0.0).astype(BF16)
        return carry

    lax.fori_loop(0, heads, mask_upstream, 0)

    peak = jnp.full((1, all_rows), -jnp.inf, F32)
    for c in range(CHUNKS):
        part = arrive(c)
        span = pl.ds(c * chunk, chunk)
        keys[span] = part
        scores[span] = dot_nt(part, q_rows[...])
        peak = jnp.maximum(peak, jnp.max(scores[span], axis=0, keepdims=True))
        if c > 0:
            hid_from_y(c).wait_recv()
            hid_to_sibling(c).start()

    hid_copy.wait()
    for copy in w_copies:
        copy.wait()
    resp = jnp.zeros((rows, 2 * HD), F32)
    for step in range(4):
        resp = resp + dot(hid[step, 0], w[y_peer(step)])
    for step in range(4):
        hid_to_sibling(step).wait_recv()
        resp = resp + dot(hid[step, 1], w[lax.rem(y + step, 4) * 2 + 1 - core])
    resp = resp.astype(BF16)
    resp_keys, resp_values = resp[:, :HD], resp[:, HD:]
    tail = pl.ds(prompt_len, rows)
    keys[tail] = resp_keys
    key_pos = lax.broadcasted_iota(jnp.int32, (rows, all_rows), 0)
    row_pos = lax.rem(lax.broadcasted_iota(jnp.int32, (rows, all_rows), 1), rows)
    visible = (key_pos <= row_pos) & (key_pos < length)
    scores[tail] = jnp.where(visible, dot_nt(resp_keys, q_rows[...]), -1e30)
    peak = jnp.maximum(peak, jnp.max(scores[tail], axis=0, keepdims=True))

    factor = scale * math.log2(math.e)
    tile = 64
    tiles = key_count // tile

    def exponents(i, total_sum):
        span = pl.ds(i * tile, tile)
        value = jnp.exp2((scores[span] - peak) * factor)
        scores[span] = value
        return total_sum + jnp.sum(value.reshape(tile // 8, 8, all_rows), axis=0)

    sums = lax.fori_loop(0, tiles, exponents, jnp.zeros((8, all_rows), F32))
    inverse = 1.0 / jnp.sum(sums, axis=0, keepdims=True)

    def normalise(i, carry):
        span = pl.ds(i * tile, tile)
        value = scores[span] * inverse
        scores[span] = value
        weights[span] = value.astype(BF16)
        return carry

    lax.fori_loop(0, tiles, normalise, 0)

    def ret_near(c):
        return along_z(ret_own.at[c], ret_a.at[c], ret_s1.at[c], ret_ra.at[c], mate)

    def ret_far(c):
        return along_z(ret_own.at[c], ret_c.at[c], ret_s2.at[c], ret_rc.at[c], far)

    def ret_opp(c):
        return along_z(ret_own.at[c], ret_b.at[c], ret_s2.at[c], ret_rb.at[c], opp)

    def ret_relayed(c):
        return along_z(ret_relay.at[c], ret_a.at[c], ret_s1.at[c], ret_ra.at[c], mate)

    def send_back(c):
        @pl.when(is_edge)
        def _():
            ret_far(c).start()
            ret_near(c).start()

        @pl.when(is_middle)
        def _():
            ret_opp(c).start()

    def grads_of_values(start, count, values):
        span = pl.ds(start, count)
        grads = dot_nt(values, u_rows[...])
        prob_grads[span] = grads
        seen = grads * weights[span].astype(F32)
        return jnp.sum(seen, axis=0, keepdims=True)

    row_dot = grads_of_values(prompt_len, rows, resp_values)
    grad_value = dot(weights[tail], u_rows[...]).astype(BF16)
    for c in range(CHUNKS):
        part = arrive(CHUNKS + c)
        span = pl.ds(c * chunk, chunk)
        row_dot = row_dot + grads_of_values(c * chunk, chunk, part)
        ret_own[c] = dot(weights[span], u_rows[...]).astype(BF16)
        send_back(c)

    def grads_of_scores(i, carry):
        span = pl.ds(i * tile, tile)
        score_grads[span] = (scores[span] * (prob_grads[span] - row_dot)).astype(BF16)
        return carry

    per_chunk = chunk // tile
    for c in range(CHUNKS):
        span = pl.ds(c * chunk, chunk)
        lax.fori_loop(c * per_chunk, (c + 1) * per_chunk, grads_of_scores, 0)
        ret_own[CHUNKS + c] = (dot(score_grads[span], q_rows[...]) * scale).astype(BF16)
        send_back(CHUNKS + c)
    lax.fori_loop(CHUNKS * per_chunk, tiles, grads_of_scores, 0)
    grad_key = (dot(score_grads[tail], q_rows[...]) * scale).astype(BF16)

    resp_grads = jnp.concatenate([grad_key, grad_value], axis=1)

    def gh_to_sibling(step):
        return along_t(
            sib_send.at[step], sib_recv.at[step], gh_ss.at[step], gh_sr.at[step], sibling
        )

    def gh_to_y(step):
        return along_t(
            y_send.at[step], y_recv.at[4 - step], gh_ys.at[step], gh_yr.at[4 - step], y_peer(step)
        )

    def gh_from_y(step):
        return along_t(
            y_send.at[step], y_recv.at[step], gh_ys.at[step], gh_yr.at[step], y_peer(step)
        )

    for step in (2, 1, 3, 0):
        shard = lax.rem(y + step, 4) * 2 + 1 - core
        sib_send[step] = dot_nt(resp_grads, w[shard]).astype(BF16)
        gh_to_sibling(step).start()

    keys_t = keys[...].T
    gq_t = dot(keys_t, score_grads[...]) * scale
    for h in range(heads):
        gq_tile[:, pl.ds(h * HD, HD)] = gq_t[:, h * rows : (h + 1) * rows].T.astype(BF16)
    gq_copy = pltpu.make_async_copy(gq_tile, gq_out, gq_sem)
    gq_copy.start()

    def hidden_terms():
        for step in (2, 1, 3, 0):
            gh_to_sibling(step).wait_recv()
            term = dot_nt(resp_grads, w[y_peer(step)]) + sib_recv[step].astype(F32)
            y_send[step] = term.astype(BF16)
            if step > 0:
                gh_to_y(step).start()

    gh_copy = pltpu.make_async_copy(gh_tile, gh_out, gh_sem)

    def hidden_sum():
        summed = y_send[0].astype(F32)
        for step in (1, 3, 2):
            gh_from_y(step).wait_recv()
            summed = summed + y_recv[step].astype(F32)
        gh_tile[...] = summed.astype(BF16)
        gh_copy.start()

    def out_copy(c):
        where = gp_out.at[1 - c // CHUNKS, pl.ds((c % CHUNKS) * chunk, chunk)]
        return pltpu.make_async_copy(ret_sum.at[c], where, out_sem.at[c])

    def kept(flag, value):
        return jnp.where(flag, value.astype(F32), 0.0)

    for c in range(total):
        @pl.when(is_middle)
        def _():
            ret_opp(c).wait_recv()
            along_z(ret_own.at[c], ret_c.at[c], ret_s2.at[c], ret_rc.at[c], far).wait_recv()
            passed = (
                kept(my_dest == mate, ret_own[c])
                + kept(opp_dest == mate, ret_b[c])
                + kept(far_dest == mate, ret_c[c])
            )
            ret_relay[c] = passed.astype(BF16)
            ret_relayed(c).start()

        ret_near(c).wait_recv()
        summed = kept(my_dest == r, ret_own[c]) + kept(is_edge | (mate_dest == r), ret_a[c])
        summed = summed + kept(is_middle & (opp_dest == r), ret_b[c])
        summed = summed + kept(is_middle & (far_dest == r), ret_c[c])
        ret_sum[c] = summed.astype(BF16)
        out_copy(c).start()
        if c == 0:
            hidden_terms()
        if c == total - 2:
            hidden_sum()

    gq_copy.wait()
    gh_copy.wait()
    for step in range(4):
        hid_to_sibling(step).wait_send()
        gh_to_sibling(step).wait_send()
        if step > 0:
            hid_to_y(step).wait_send()
            gh_to_y(step).wait_send()
    for c in range(total):
        fwd_near(c).wait_send()
        fwd_opp(c).wait_send()
        ret_near(c).wait_send()
        ret_opp(c).wait_send()
        out_copy(c).wait()


def local(hidden, queries, out_grad, w_key, w_value, prompt_kv, block_dest, resp_len):
    rows, q_cols = queries.shape
    shard_cols = hidden.shape[1]
    shards = w_key.shape[0] // shard_cols
    kv_cols = w_key.shape[1]
    prompt_len = prompt_kv.shape[2]
    chunk = prompt_len // CHUNKS
    total = 2 * CHUNKS
    all_rows = q_cols // HD * rows
    heads = q_cols // HD
    key_count = prompt_len + rows
    dma = pltpu.SemaphoreType.DMA
    part = pltpu.VMEM((total, chunk, kv_cols), BF16)
    shard = (rows, shard_cols)
    any_space = pl.BlockSpec(memory_space=pl.ANY)
    smem = pl.BlockSpec(memory_space=pltpu.SMEM)
    scratch = (
        [part] * 11
        + [pltpu.VMEM((all_rows, HD), BF16)] * 2
        + [
            pltpu.VMEM((key_count, HD), BF16),
            pltpu.VMEM((key_count, all_rows), F32),
            pltpu.VMEM((key_count, all_rows), F32),
            pltpu.VMEM((key_count, all_rows), BF16),
            pltpu.VMEM((key_count, all_rows), BF16),
            pltpu.VMEM((shards, shard_cols, 2 * kv_cols), BF16),
            pltpu.VMEM((4, 2) + shard, BF16),
        ]
        + [pltpu.VMEM((4,) + shard, BF16)] * 4
        + [pltpu.VMEM((rows, q_cols), BF16), pltpu.VMEM(shard, BF16)]
        + [dma((total,))] * 10
        + [dma((4,))] * 8
        + [dma((total,)), dma((heads,)), dma((heads,)), dma((2,)), dma, dma((total,)), dma, dma]
    )
    grad_query, grad_hidden, grad_prompt = pl.pallas_call(
        kernel,
        out_shape=(
            jax.ShapeDtypeStruct(queries.shape, BF16),
            jax.ShapeDtypeStruct(hidden.shape, BF16),
            jax.ShapeDtypeStruct(prompt_kv.shape[1:], BF16),
        ),
        in_specs=[smem] * 2 + [any_space] * 6,
        out_specs=[any_space] * 3,
        scratch_shapes=scratch,
        compiler_params=pltpu.CompilerParams(
            collective_id=0, has_side_effects=True, vmem_limit_bytes=48 * 1024 * 1024
        ),
        name="attention_backward",
    )(
        block_dest, resp_len, hidden, queries, out_grad,
        w_key.reshape(shards, shard_cols, kv_cols), w_value.reshape(shards, shard_cols, kv_cols),
        prompt_kv[0],
    )
    return grad_query, grad_hidden, grad_prompt[None]


def solution(mesh):
    return jax.shard_map(
        local,
        mesh=mesh,
        in_specs=(
            P("dp", "tensor"),
            P("dp", "tensor"),
            P("dp", "tensor"),
            P(None, "tensor"),
            P(None, "tensor"),
            P("dp", None, None, "tensor"),
            P(),
            P(),
        ),
        out_specs=(P("dp", "tensor"), P("dp", "tensor"), P("dp", None, None, "tensor")),
        check_vma=False,
    )
```

time: 381 us -> 70.8 us (0.19)
  waiting for transfers between devices: 149 us -> 0 us
  starting transfers between devices: 89 us -> 0 us
  Pallas kernels: 0 us -> 59.8 us
  between operations: 47.9 us -> 0.66 us
  matrix products: 38.9 us -> 0 us
  other arithmetic: 26.4 us -> 0 us
  local copies, waits for them, and re-layouts: 27.8 us -> 9.95 us
    psum x1 -> x0, waiting for transfers between devices: 95.5 us -> none  [local(): lax.psum(partial_value.astype(jnp.bfloat16), 'tensor').astype(jnp.float32)]
    ppermute x12 -> x0, starting transfers between devices: 89 us -> none  [from_behind(): return lax.ppermute(block, axis, route)]
    pallas_call x0 -> x1, Pallas kernels: none -> 59.8 us  [local(): pl.pallas_call(kernel, out_shape=(jax.ShapeDtypeStruct(queries.shape, BF1...]
    ppermute x12 -> x0, waiting for transfers between devices: 30.7 us -> none  [from_behind(): return lax.ppermute(block, axis, route)]
    dot_general x19 -> x0, matrix products: 24.3 us -> none  [the longest x3 4.81 us: block_grads(): jnp.einsum('gij,igd->jd', score_grad, query_head, preferred_element_type=...]
    all_gather x1 -> x0, waiting for transfers between devices: 22 us -> none  [local(): full_hidden = lax.all_gather(hidden, 'tensor', axis=1, tiled=True)]
    sub x3 -> x0, matrix products: 14.6 us -> none  [block_grads(): exponent = jnp.exp(scores - row_peak)]
    convert_element_type x5 -> x0, other arithmetic: 13 us -> none  [the longest x3 9.32 us: block_grads(): weights = softmax_out.astype(jnp.bfloat16)]
  transfers between devices with their start and end apart: 14 -> 0, of which waited for: 5 -> 0; matrix products, arithmetic and copies ran while one was open for 7% -> 0% of each run, Pallas kernels for 0% -> 0%
where the time goes in v1:
time: 70.8 us; the launch traced here: 70.5 us
  Pallas kernels  59.8 us (84%)
  local copies, waits for them, and re-layouts  9.95 us (14%)
    pallas_call x1, Pallas kernels, local(): pl.pallas_call(kernel, out_shape=(jax.ShapeDtypeStruct(queries.shape, BF1...  59.8 us
    unnamed x19, local copies, waits for them, and re-layouts  9.95 us

profile of v1, /device:TPU:1, one launch (start us, length us, event | category | flops | bytes accessed | tf_op | source)
XLA Modules:
  0.0 70.5 jit_solution(7104470516046254417)
XLA Ops:
  0.6 0.0 copy-start
  0.6 1.3 %copy-done = bf16[5120,128]{1,0:T(8,128)(2,1)S(1)} copy-done((bf16[5120,128]{1,0:T(8,128)(2,1)S(1)}, bf16[5120,128]{1,0:T(8,128)(2,1)}, u32[]{:S(2)}) %copy-start) | copy-done | bytes 1310744
  2.0 0.0 copy-start.1
  2.0 1.3 %copy-done.1 = bf16[5120,128]{1,0:T(8,128)(2,1)S(1)} copy-done((bf16[5120,128]{1,0:T(8,128)(2,1)S(1)}, bf16[5120,128]{1,0:T(8,128)(2,1)}, u32[]{:S(2)}) %copy-start.1) | copy-done | bytes 1310744
  3.3 0.0 copy-start.2
  3.3 1.0 %copy-done.2 = bf16[1,2,1024,128]{3,2,1,0:T(8,128)(2,1)S(1)} copy-done((bf16[1,2,1024,128]{3,2,1,0:T(8,128)(2,1)S(1)}, bf16[1,2,1024,128]{3,2,1,0:T(8,128)(2,1)}, u32[]{:S(2)}) %copy-start.2) | copy-done | bytes 524312
  4.3 0.0 copy-start.3
  4.3 0.9 %copy-done.3 = bf16[128,1024]{1,0:T(8,128)(2,1)S(1)} copy-done((bf16[128,1024]{1,0:T(8,128)(2,1)S(1)}, bf16[128,1024]{1,0:T(8,128)(2,1)}, u32[]{:S(2)}) %copy-start.3) | copy-done | bytes 262168
  5.3 0.0 copy-start.4
  5.3 0.9 %copy-done.4 = bf16[128,1024]{1,0:T(8,128)(2,1)S(1)} copy-done((bf16[128,1024]{1,0:T(8,128)(2,1)S(1)}, bf16[128,1024]{1,0:T(8,128)(2,1)}, u32[]{:S(2)}) %copy-start.4) | copy-done | bytes 262168
  6.2 0.0 copy-start.5
  6.2 0.9 %copy-done.5 = bf16[128,640]{1,0:T(8,128)(2,1)S(1)} copy-done((bf16[128,640]{1,0:T(8,128)(2,1)S(1)}, bf16[128,640]{1,0:T(8,128)(2,1)}, u32[]{:S(2)}) %copy-start.5) | copy-done | bytes 163864
  7.1 0.0 copy-start.6
  7.1 0.7 copy-done.6
  7.8 0.0 copy-start.7
  7.8 0.7 copy-done.7
  8.4 59.8 %attention_backward.1 = (bf16[128,1024]{1,0:T(8,128)(2,1)S(1)}, bf16[128,640]{1,0:T(8,128)(2,1)S(1)}, bf16[2,1024,128]{2,1,0:T(8,128)(2,1)S(1)}) custom-call(s32[64]{0:T(128)S(1)} %copy-done.6, s32[64]{0:T(128)S(1)} %copy-done.7, bf16[128,640]{1,0:T(8,128)(2,1)S(1)} %copy-done.5, bf16[128,1024]{1,0:T(8,128)(2,1)S(1)} %copy-done.3, ...), custom_call_target="tpu_custom_call" | custom-call | tf_op jit(solution)/shard_map/attention_backward/pallas_call | solution.py:424
  68.3 0.7 %copy.14 = bf16[128,1024]{1,0:T(8,128)(2,1)} copy(bf16[128,1024]{1,0:T(8,128)(2,1)S(1)} %get-tuple-element.12) | data formatting | bytes 524288
  69.0 0.7 copy.15
  69.7 0.8 %copy.16 = bf16[1,2,1024,128]{3,2,1,0:T(8,128)(2,1)} copy(bf16[1,2,1024,128]{3,2,1,0:T(8,128)(2,1)S(1)} %bitcast.6) | data formatting | bytes 1048576
Async XLA Ops:
  0.6 1.3 %copy-start = (bf16[5120,128]{1,0:T(8,128)(2,1)S(1)}, bf16[5120,128]{1,0:T(8,128)(2,1)}, u32[]{:S(2)}) copy-start(bf16[5120,128]{1,0:T(8,128)(2,1)} %param.11) | copy-start | bytes 3932164
  2.0 1.3 %copy-start.1 = (bf16[5120,128]{1,0:T(8,128)(2,1)S(1)}, bf16[5120,128]{1,0:T(8,128)(2,1)}, u32[]{:S(2)}) copy-start(bf16[5120,128]{1,0:T(8,128)(2,1)} %param.12) | copy-start | bytes 3932164
  3.3 1.0 %copy-start.2 = (bf16[1,2,1024,128]{3,2,1,0:T(8,128)(2,1)S(1)}, bf16[1,2,1024,128]{3,2,1,0:T(8,128)(2,1)}, u32[]{:S(2)}) copy-start(bf16[1,2,1024,128]{3,2,1,0:T(8,128)(2,1)} %param.13) | copy-start | bytes 1572868
  4.3 0.9 %copy-start.3 = (bf16[128,1024]{1,0:T(8,128)(2,1)S(1)}, bf16[128,1024]{1,0:T(8,128)(2,1)}, u32[]{:S(2)}) copy-start(bf16[128,1024]{1,0:T(8,128)(2,1)} %q_ref.1) | copy-start | bytes 786436
  5.3 0.9 %copy-start.4 = (bf16[128,1024]{1,0:T(8,128)(2,1)S(1)}, bf16[128,1024]{1,0:T(8,128)(2,1)}, u32[]{:S(2)}) copy-start(bf16[128,1024]{1,0:T(8,128)(2,1)} %u_ref.1) | copy-start | bytes 786436
  6.2 0.9 %copy-start.5 = (bf16[128,640]{1,0:T(8,128)(2,1)S(1)}, bf16[128,640]{1,0:T(8,128)(2,1)}, u32[]{:S(2)}) copy-start(bf16[128,640]{1,0:T(8,128)(2,1)} %hidden_ref.1) | copy-start | bytes 491524
  7.1 0.7 copy-start.6
  7.8 0.7 copy-start.7

commit v2 on v1

--- a/solution.py
+++ b/solution.py
@@ -32,6 +32,7 @@
     fwd_s1, fwd_s2, fwd_ra, fwd_rb, fwd_rc, ret_s1, ret_s2, ret_ra, ret_rb, ret_rc,
     hid_ys, hid_yr, hid_ss, hid_sr, gh_ss, gh_sr, gh_ys, gh_yr,
     own_sem, q_sem, u_sem, w_sem, hid_sem, out_sem, gq_sem, gh_sem,
+    dests, lengths, dest_sem, len_sem,
 ):
     rows = q_ref.shape[0]
     heads = q_ref.shape[1] // HD
@@ -90,6 +91,10 @@
     )
     hid_copy = pltpu.make_async_copy(hidden_ref, hid.at[0, 0], hid_sem)
 
+    dest_copy = pltpu.make_async_copy(dest_ref, dests, dest_sem)
+    len_copy = pltpu.make_async_copy(len_ref, lengths, len_sem)
+    dest_copy.start()
+    len_copy.start()
     for h in range(heads):
         for copy in head_copies(h):
             copy.start()
@@ -152,12 +157,13 @@
     for step in (2, 1, 3):
         hid_to_y(step).start()
 
-    dest_of = [dest_ref[base + place] - base for place in range(GROUP)]
-    my_dest = dest_ref[me] - base
-    mate_dest = dest_ref[base + mate] - base
-    opp_dest = dest_ref[base + opp] - base
-    far_dest = dest_ref[base + far] - base
-    length = len_ref[me]
+    dest_copy.wait()
+    len_copy.wait()
+    my_dest = dests[me] - base
+    mate_dest = dests[base + mate] - base
+    opp_dest = dests[base + opp] - base
+    far_dest = dests[base + far] - base
+    length = lengths[me]
     use_own = my_dest == r
     use_a = is_edge | (my_dest == mate)
     use_b = my_dest == opp
@@ -401,8 +407,7 @@
     dma = pltpu.SemaphoreType.DMA
     part = pltpu.VMEM((total, chunk, kv_cols), BF16)
     shard = (rows, shard_cols)
-    any_space = pl.BlockSpec(memory_space=pl.ANY)
-    smem = pl.BlockSpec(memory_space=pltpu.SMEM)
+    hbm = pl.BlockSpec(memory_space=pltpu.HBM)
     scratch = (
         [part] * 11
         + [pltpu.VMEM((all_rows, HD), BF16)] * 2
@@ -420,6 +425,7 @@
         + [dma((total,))] * 10
         + [dma((4,))] * 8
         + [dma((total,)), dma((heads,)), dma((heads,)), dma((2,)), dma, dma((total,)), dma, dma]
+        + [pltpu.SMEM(block_dest.shape, jnp.int32), pltpu.SMEM(resp_len.shape, jnp.int32), dma, dma]
     )
     grad_query, grad_hidden, grad_prompt = pl.pallas_call(
         kernel,
@@ -428,11 +434,11 @@
             jax.ShapeDtypeStruct(hidden.shape, BF16),
             jax.ShapeDtypeStruct(prompt_kv.shape[1:], BF16),
         ),
-        in_specs=[smem] * 2 + [any_space] * 6,
-        out_specs=[any_space] * 3,
+        in_specs=[hbm] * 8,
+        out_specs=[hbm] * 3,
         scratch_shapes=scratch,
         compiler_params=pltpu.CompilerParams(
-            collective_id=0, has_side_effects=True, vmem_limit_bytes=48 * 1024 * 1024
+            collective_id=0, has_side_effects=True, vmem_limit_bytes=60 * 1024 * 1024
         ),
         name="attention_backward",
     )(

time: 70.8 us -> 64.5 us (0.911)
  local copies, waits for them, and re-layouts: 9.95 us -> 5.13 us
  Pallas kernels: 59.8 us -> 58.5 us
    unnamed x19 -> x3, local copies, waits for them, and re-layouts: 9.95 us -> 5.13 us
    pallas_call x1, Pallas kernels: 59.8 us -> 58.5 us  [local(): pl.pallas_call(kernel, out_shape=(jax.ShapeDtypeStruct(queries.shape, BF1...]
where the time goes in v2:
time: 64.5 us; the launch traced here: 64.3 us
  Pallas kernels  58.5 us (91%)
  local copies, waits for them, and re-layouts  5.13 us (8%)
    pallas_call x1, Pallas kernels, local(): pl.pallas_call(kernel, out_shape=(jax.ShapeDtypeStruct(queries.shape, BF1...  58.5 us
    unnamed x3, local copies, waits for them, and re-layouts  5.13 us

profile of v2, /device:TPU:1, one launch (start us, length us, event | category | flops | bytes accessed | tf_op | source)
XLA Modules:
  0.0 64.3 jit_solution(17246069170394458751)
XLA Ops:
  0.6 58.5 %attention_backward.1 = (bf16[128,1024]{1,0:T(8,128)(2,1)}, bf16[128,640]{1,0:T(8,128)(2,1)}, bf16[2,1024,128]{2,1,0:T(8,128)(2,1)}) custom-call(s32[64]{0:T(128)} %dest_ref.1, s32[64]{0:T(128)} %len_ref.1, bf16[128,640]{1,0:T(8,128)(2,1)} %hidden_ref.1, bf16[128,1024]{1,0:T(8,128)(2,1)} %q_ref.1, bf16[128,1024]{1,0:T(8,128)(2,1)} %u_ref.1, ...), custom_call_target="tpu_custom_call" | custom-call | tf_op jit(solution)/shard_map/attention_backward/pallas_call | solution.py:430
  59.2 1.7 %copy.14 = bf16[128,1024]{1,0:T(8,128)(2,1)} copy(bf16[128,1024]{1,0:T(8,128)(2,1)} %get-tuple-element.12) | data formatting | bytes 524288
  60.9 1.6 %copy.15 = bf16[128,640]{1,0:T(8,128)(2,1)} copy(bf16[128,640]{1,0:T(8,128)(2,1)} %get-tuple-element.13) | data formatting | bytes 327680
  62.5 1.9 %copy.16 = bf16[1,2,1024,128]{3,2,1,0:T(8,128)(2,1)} copy(bf16[1,2,1024,128]{3,2,1,0:T(8,128)(2,1)} %bitcast.6) | data formatting | bytes 1048576

commit v3 on v2

--- a/solution.py
+++ b/solution.py
@@ -26,12 +26,12 @@
 def kernel(
     dest_ref, len_ref, hidden_ref, q_ref, u_ref, wk_ref, wv_ref, kv_ref,
     gq_out, gh_out, gp_out,
-    own, fwd_a, fwd_b, fwd_c, fwd_relay, ret_own, ret_a, ret_b, ret_c, ret_relay, ret_sum,
+    own, fwd_a, fwd_b, fwd_c, fwd_relay, ret_own, ret_a, ret_b, ret_c, ret_relay,
     q_rows, u_rows, keys, scores, prob_grads, weights, score_grads,
-    w, hid, sib_send, sib_recv, y_send, y_recv, gq_tile, gh_tile,
+    w, hid, sib_send, sib_recv, y_send, y_recv,
     fwd_s1, fwd_s2, fwd_ra, fwd_rb, fwd_rc, ret_s1, ret_s2, ret_ra, ret_rb, ret_rc,
     hid_ys, hid_yr, hid_ss, hid_sr, gh_ss, gh_sr, gh_ys, gh_yr,
-    own_sem, q_sem, u_sem, w_sem, hid_sem, out_sem, gq_sem, gh_sem,
+    own_sem, q_sem, u_sem, w_sem, hid_sem,
     dests, lengths, dest_sem, len_sem,
 ):
     rows = q_ref.shape[0]
@@ -324,9 +324,7 @@
     keys_t = keys[...].T
     gq_t = dot(keys_t, score_grads[...]) * scale
     for h in range(heads):
-        gq_tile[:, pl.ds(h * HD, HD)] = gq_t[:, h * rows : (h + 1) * rows].T.astype(BF16)
-    gq_copy = pltpu.make_async_copy(gq_tile, gq_out, gq_sem)
-    gq_copy.start()
+        gq_out[:, pl.ds(h * HD, HD)] = gq_t[:, h * rows : (h + 1) * rows].T.astype(BF16)
 
     def hidden_terms():
         for step in (2, 1, 3, 0):
@@ -336,19 +334,12 @@
             if step > 0:
                 gh_to_y(step).start()
 
-    gh_copy = pltpu.make_async_copy(gh_tile, gh_out, gh_sem)
-
     def hidden_sum():
         summed = y_send[0].astype(F32)
         for step in (1, 3, 2):
             gh_from_y(step).wait_recv()
             summed = summed + y_recv[step].astype(F32)
-        gh_tile[...] = summed.astype(BF16)
-        gh_copy.start()
-
-    def out_copy(c):
-        where = gp_out.at[1 - c // CHUNKS, pl.ds((c % CHUNKS) * chunk, chunk)]
-        return pltpu.make_async_copy(ret_sum.at[c], where, out_sem.at[c])
+        gh_out[...] = summed.astype(BF16)
 
     def kept(flag, value):
         return jnp.where(flag, value.astype(F32), 0.0)
@@ -370,15 +361,12 @@
         summed = kept(my_dest == r, ret_own[c]) + kept(is_edge | (mate_dest == r), ret_a[c])
         summed = summed + kept(is_middle & (opp_dest == r), ret_b[c])
         summed = summed + kept(is_middle & (far_dest == r), ret_c[c])
-        ret_sum[c] = summed.astype(BF16)
-        out_copy(c).start()
+        gp_out[1 - c // CHUNKS, pl.ds((c % CHUNKS) * chunk, chunk)] = summed.astype(BF16)
         if c == 0:
             hidden_terms()
         if c == total - 2:
             hidden_sum()
 
-    gq_copy.wait()
-    gh_copy.wait()
     for step in range(4):
         hid_to_sibling(step).wait_send()
         gh_to_sibling(step).wait_send()
@@ -390,7 +378,30 @@
         fwd_opp(c).wait_send()
         ret_near(c).wait_send()
         ret_opp(c).wait_send()
-        out_copy(c).wait()
+
+
+def write_kernel(a_ref, b_ref, c_ref, a_out, b_out, c_out, sems):
+    copies = [
+        pltpu.make_async_copy(src, dst, sems.at[i])
+        for i, (src, dst) in enumerate(((c_ref, c_out), (a_ref, a_out), (b_ref, b_out)))
+    ]
+    for copy in copies:
+        copy.start()
+    for copy in copies:
+        copy.wait()
+
+
+def write_out(*arrays):
+    anywhere = pl.BlockSpec(memory_space=pl.ANY)
+    return pl.pallas_call(
+        write_kernel,
+        out_shape=tuple(jax.ShapeDtypeStruct(a.shape, a.dtype) for a in arrays),
+        in_specs=[anywhere] * 3,
+        out_specs=[anywhere] * 3,
+        scratch_shapes=[pltpu.SemaphoreType.DMA((3,))],
+        compiler_params=pltpu.CompilerParams(vmem_limit_bytes=1024 * 1024),
+        name="write_out",
+    )(*arrays)
 
 
 def local(hidden, queries, out_grad, w_key, w_value, prompt_kv, block_dest, resp_len):
@@ -409,7 +420,7 @@
     shard = (rows, shard_cols)
     hbm = pl.BlockSpec(memory_space=pltpu.HBM)
     scratch = (
-        [part] * 11
+        [part] * 10
         + [pltpu.VMEM((all_rows, HD), BF16)] * 2
         + [
             pltpu.VMEM((key_count, HD), BF16),
@@ -421,21 +432,20 @@
             pltpu.VMEM((4, 2) + shard, BF16),
         ]
         + [pltpu.VMEM((4,) + shard, BF16)] * 4
-        + [pltpu.VMEM((rows, q_cols), BF16), pltpu.VMEM(shard, BF16)]
         + [dma((total,))] * 10
         + [dma((4,))] * 8
-        + [dma((total,)), dma((heads,)), dma((heads,)), dma((2,)), dma, dma((total,)), dma, dma]
+        + [dma((total,)), dma((heads,)), dma((heads,)), dma((2,)), dma]
         + [pltpu.SMEM(block_dest.shape, jnp.int32), pltpu.SMEM(resp_len.shape, jnp.int32), dma, dma]
     )
     grad_query, grad_hidden, grad_prompt = pl.pallas_call(
         kernel,
         out_shape=(
-            jax.ShapeDtypeStruct(queries.shape, BF16),
-            jax.ShapeDtypeStruct(hidden.shape, BF16),
-            jax.ShapeDtypeStruct(prompt_kv.shape[1:], BF16),
+            pltpu.VMEM(queries.shape, BF16),
+            pltpu.VMEM(hidden.shape, BF16),
+            pltpu.VMEM(prompt_kv.shape[1:], BF16),
         ),
         in_specs=[hbm] * 8,
-        out_specs=[hbm] * 3,
+        out_specs=[pl.BlockSpec(memory_space=pltpu.VMEM)] * 3,
         scratch_shapes=scratch,
         compiler_params=pltpu.CompilerParams(
             collective_id=0, has_side_effects=True, vmem_limit_bytes=60 * 1024 * 1024
@@ -446,7 +456,7 @@
         w_key.reshape(shards, shard_cols, kv_cols), w_value.reshape(shards, shard_cols, kv_cols),
         prompt_kv[0],
     )
-    return grad_query, grad_hidden, grad_prompt[None]
+    return write_out(grad_query, grad_hidden, grad_prompt[None])
 
 
 def solution(mesh):

time: 64.5 us -> 59.6 us (0.924)
  local copies, waits for them, and re-layouts: 5.13 us -> 0 us
    unnamed x3 -> x0, local copies, waits for them, and re-layouts: 5.13 us -> none
    pallas_call x1 -> x2, Pallas kernels: 58.5 us -> 58.9 us  [the longest x1 57.9 us: local(): pl.pallas_call(kernel, out_shape=(pltpu.VMEM(queries.shape, BF16), pltpu....]
where the time goes in v3:
time: 59.6 us; the launch traced here: 59.5 us
  Pallas kernels  58.9 us (99%)
  between operations  0.64 us (1%)
    pallas_call x1, Pallas kernels, local(): pl.pallas_call(kernel, out_shape=(pltpu.VMEM(queries.shape, BF16), pltpu....  57.9 us

profile of v3, /device:TPU:1, one launch (start us, length us, event | category | flops | bytes accessed | tf_op | source)
XLA Modules:
  0.0 59.5 jit_solution(12885425794108016757)
XLA Ops:
  0.6 57.9 %attention_backward.1 = (bf16[128,1024]{1,0:T(8,128)(2,1)S(1)}, bf16[128,640]{1,0:T(8,128)(2,1)S(1)}, bf16[2,1024,128]{2,1,0:T(8,128)(2,1)S(1)}) custom-call(s32[64]{0:T(128)} %dest_ref.1, s32[64]{0:T(128)} %len_ref.1, bf16[128,640]{1,0:T(8,128)(2,1)} %hidden_ref.1, bf16[128,1024]{1,0:T(8,128)(2,1)} %q_ref.1, bf16[128,1024]{1,0:T(8,128)(2,1)} %u_ref.1, ...), custom_call_target="tpu_custom_call" | custom-call | tf_op jit(solution)/shard_map/attention_backward/pallas_call | solution.py:440
  58.5 1.0 %write_out.1 = (bf16[128,1024]{1,0:T(8,128)(2,1)}, bf16[128,640]{1,0:T(8,128)(2,1)}, bf16[1,2,1024,128]{3,2,1,0:T(8,128)(2,1)}) custom-call(bf16[128,1024]{1,0:T(8,128)(2,1)S(1)} %get-tuple-element.6.a_ref, bf16[128,640]{1,0:T(8,128)(2,1)S(1)} %get-tuple-element.7.b_ref, bf16[1,2,1024,128]{3,2,1,0:T(8,128)(2,1)S(1)} %bitcast.4), custom_call_target="tpu_custom_call" | custom-call | tf_op jit(solution)/shard_map/write_out/pallas_call | solution.py:396

commit v4 on v3

v4 whole, which is shorter than its diff:
```python
import math

import jax
import jax.numpy as jnp
from jax import lax
from jax.experimental import pallas as pl
from jax.experimental.pallas import tpu as pltpu
from jax.sharding import PartitionSpec as P

HD = 128
GROUP = 4
CHUNKS = 4
MESH = pl.DeviceIdType.MESH
BF16 = jnp.bfloat16
F32 = jnp.float32


def dot_nt(a, b):
    return lax.dot_general(a, b, (((1,), (1,)), ((), ())), preferred_element_type=F32)


def dot(a, b):
    return jnp.dot(a, b, preferred_element_type=F32)


def kernel(
    dest_ref, len_ref, hidden_ref, q_ref, u_ref, wk_ref, wv_ref, kv_ref,
    gq_out, gh_out, gp_out,
    own, edge_kv, pass_kv, pass_in, relay_kv, relay_in, pg_own, pg_guest, pg_edge, pg_far, pg_relay, pg_back,
    q_rows, u_rows, guest_q, guest_u, gq_own, gq_guest, gq_back,
    keys, guest_keys, scores, guest_scores, prob_grads, weights, score_grads, resp_kv, resp_queries, resp_scores, resp_prob_grads, resp_score_grads, resp_grads,
    stat_resp, stat_guest, fin_own, fin_guest, fin_back, local_own, local_guest,
    w, hid, sib_send, sib_recv, y_send, y_recv, y_half,
    kv_s, kv_r, q_s, q_r, pass_s, pass_r, relay_s, relay_r, pe_s, pe_r, far_s, far_r, back_s, back_r,
    res_s, res_r, stat_s, stat_r, hid_ys, hid_yr, hid_ss, hid_sr, gh_ss, gh_sr, gh_ys, gh_yr,
    own_sem, qu_sem, w_sem, hid_sem, dests, lengths, small_sem,
):
    rows = q_ref.shape[0]
    heads = q_ref.shape[1] // HD
    all_rows = heads * rows
    prompt_len = kv_ref.shape[1]
    chunk = prompt_len // CHUNKS
    total = 2 * CHUNKS
    scale = 1.0 / math.sqrt(HD)
    factor = scale * math.log2(math.e)
    tile = 64

    me = lax.axis_index("dp")
    r = lax.rem(me, GROUP)
    base = me - r
    mate = r + 1 - 2 * lax.rem(r, 2)
    opp = GROUP - 1 - r
    far = lax.rem(r + 2, GROUP)
    is_edge = (r == 0) | (r == GROUP - 1)
    is_middle = (r == 1) | (r == GROUP - 2)
    tensor = lax.axis_index("tensor")
    core = lax.rem(tensor, 2)
    y = tensor // 2
    sibling = tensor + 1 - 2 * core

    def y_peer(step):
        return lax.rem(y + step, 4) * 2 + core

    def along_z(src, dst, send, recv, place):
        return pltpu.make_async_remote_copy(
            src_ref=src, dst_ref=dst, send_sem=send, recv_sem=recv,
            device_id={"dp": base + place}, device_id_type=MESH,
        )

    def along_t(src, dst, send, recv, place):
        return pltpu.make_async_remote_copy(
            src_ref=src, dst_ref=dst, send_sem=send, recv_sem=recv,
            device_id={"tensor": place}, device_id_type=MESH,
        )

    def kv_part(c):
        return kv_ref.at[c // CHUNKS, pl.ds((c % CHUNKS) * chunk, chunk)]

    def own_copy(c):
        return pltpu.make_async_copy(kv_part(c), own.at[c], own_sem.at[c])

    def head_copies(h):
        span = pl.ds(h * HD, HD)
        place = pl.ds(h * rows, rows)
        return (
            pltpu.make_async_copy(q_ref.at[:, span], q_rows.at[place], qu_sem.at[h]),
            pltpu.make_async_copy(u_ref.at[:, span], u_rows.at[place], qu_sem.at[heads + h]),
        )

    w_copies = (
        pltpu.make_async_copy(wk_ref, w.at[:, :, pl.ds(0, HD)], w_sem.at[0]),
        pltpu.make_async_copy(wv_ref, w.at[:, :, pl.ds(HD, HD)], w_sem.at[1]),
    )
    hid_copy = pltpu.make_async_copy(hidden_ref, hid.at[0, 0], hid_sem)
    dest_copy = pltpu.make_async_copy(dest_ref, dests, small_sem.at[0])
    len_copy = pltpu.make_async_copy(len_ref, lengths, small_sem.at[1])

    dest_copy.start()
    len_copy.start()
    for h in range(heads):
        for copy in head_copies(h):
            copy.start()
    for c in range(total):
        own_copy(c).start()
    hid_copy.start()
    for copy in w_copies:
        copy.start()

    barrier = pltpu.get_barrier_semaphore()
    for step in range(1, GROUP):
        pl.semaphore_signal(
            barrier, inc=1, device_id={"dp": base + lax.rem(r + step, GROUP)}, device_id_type=MESH
        )
        pl.semaphore_signal(
            barrier, inc=1, device_id={"tensor": y_peer(step)}, device_id_type=MESH
        )
    pl.semaphore_signal(barrier, inc=1, device_id={"tensor": sibling}, device_id_type=MESH)

    dest_copy.wait()
    len_copy.wait()
    my_dest = dests[me] - base
    mate_dest = dests[base + mate] - base
    opp_dest = dests[base + opp] - base
    far_dest = dests[base + far] - base
    length = lengths[me]
    in_half = is_edge | (my_dest == r) | (my_dest == mate)

    for h in range(heads):
        for copy in head_copies(h):
            copy.wait()

    def mask_upstream(h, carry):
        place = pl.ds(h * rows, rows)
        live = lax.broadcasted_iota(jnp.int32, (rows, HD), 0) < length
        u_rows[place] = jnp.where(live, u_rows[place].astype(F32), 0.0).astype(BF16)
        return carry

    lax.fori_loop(0, heads, mask_upstream, 0)
    pl.semaphore_wait(barrier, 2 * (GROUP - 1) + 1)

    def edge_send(c):
        return along_z(own.at[c], edge_kv.at[c], kv_s.at[c], kv_r.at[c], mate)

    def row_part(c):
        return pl.ds(c * (all_rows // CHUNKS), all_rows // CHUNKS)

    def query_send(c):
        src, dst = (q_rows, guest_q) if c < CHUNKS else (u_rows, guest_u)
        place = row_part(c % CHUNKS)
        return along_z(src.at[place], dst.at[place], q_s.at[c], q_r.at[c], opp)

    def pass_send(c):
        return along_z(pass_kv.at[c], pass_in.at[c], pass_s.at[c], pass_r.at[c], opp)

    def relay_send(c):
        return along_z(relay_kv.at[c], relay_in.at[c], relay_s.at[c], relay_r.at[c], mate)

    def stat_send():
        return along_z(stat_resp, stat_guest, stat_s.at[0], stat_r.at[0], opp)

    def fin_send():
        return along_z(fin_guest, fin_back, stat_s.at[1], stat_r.at[1], opp)

    def result_send(c):
        place = row_part(c)
        return along_z(gq_guest.at[place], gq_back.at[place], res_s.at[c], res_r.at[c], opp)

    def pg_edge_send(c):
        return along_z(pg_own.at[c], pg_edge.at[c], pe_s.at[c], pe_r.at[c], mate)

    def pg_far_send(c):
        return along_z(pg_edge.at[c], pg_far.at[c], far_s.at[c], far_r.at[c], opp)

    def pg_back_send(c):
        return along_z(pg_relay.at[c], pg_back.at[c], back_s.at[c], back_r.at[c], mate)

    @pl.when(is_edge)
    def _():
        for c in range(total):
            own_copy(c).wait()
            edge_send(c).start()

    @pl.when(is_middle)
    def _():
        for c in range(2):
            query_send(c).start()
        for c in range(total):
            own_copy(c).wait()

    half = rows // 2

    def hid_to_y(step):
        return along_t(
            hidden_ref, hid.at[4 - step, 0], hid_ys.at[step], hid_yr.at[4 - step], y_peer(step)
        )

    def hid_from_y(step):
        return along_t(hidden_ref, hid.at[step, 0], hid_ys.at[step], hid_yr.at[step], y_peer(step))

    def hid_onward(step):
        place = pl.ds(0 if step == 3 else half, half)
        slot = 0 if step == 3 else 2
        return along_t(
            hid.at[step, 0, place], hid.at[2, 0, place], hid_ys.at[slot], hid_yr.at[slot], y_peer(4 - step)
        )

    def hid_to_sibling(step):
        src = hidden_ref if step == 0 else hid.at[step, 0]
        return along_t(src, hid.at[step, 1], hid_ss.at[step], hid_sr.at[step], sibling)

    for step in (1, 3):
        hid_to_y(step).start()
    hid_to_sibling(0).start()

    def attend_scores(q, key_part, chunks, scores, keys, local):
        for c in chunks:
            part = key_part(c)
            span = pl.ds(c * chunk, chunk)
            keys[span] = part
            scores[span] = dot_nt(part, q[...])
            peak = jnp.max(scores[span], axis=0, keepdims=True)
            local[0:1] = peak if c == 0 else jnp.maximum(local[0:1], peak)

    def attend_exponents(scores, local):
        peak = local[0:1]

        def exponents(i, total_sum):
            span = pl.ds(i * tile, tile)
            value = jnp.exp2((scores[span] - peak) * factor)
            scores[span] = value
            return total_sum + jnp.sum(value.reshape(tile // 8, 8, all_rows), axis=0)

        sums = lax.fori_loop(0, prompt_len // tile, exponents, jnp.zeros((8, all_rows), F32))
        local[1:2] = jnp.sum(sums, axis=0, keepdims=True)

    def attend_values(u, scores, local, stats, pg, after_values, between):
        peak = jnp.maximum(local[0:1], stats[0:1])
        fade = jnp.exp2((local[0:1] - peak) * factor)
        resp_fade = jnp.exp2((stats[0:1] - peak) * factor)
        inverse = 1.0 / (local[1:2] * fade + stats[1:2] * resp_fade)
        share = fade * inverse

        def normalise(i, carry):
            span = pl.ds(i * tile, tile)
            value = scores[span] * share
            scores[span] = value
            weights[span] = value.astype(BF16)
            return carry

        lax.fori_loop(0, prompt_len // tile, normalise, 0)
        between()
        local[2:3] = peak
        local[3:4] = inverse
        local[4:5] = stats[2:3] * resp_fade * inverse
        for c in range(CHUNKS):
            pg[c] = dot(weights[pl.ds(c * chunk, chunk)], u[...]).astype(BF16)
            after_values(c)

    def attend_dot(u, value_part, local, fin):
        row_dot = local[4:5]
        for c in range(CHUNKS):
            span = pl.ds(c * chunk, chunk)
            grads = dot_nt(value_part(c), u[...])
            prob_grads[span] = grads
            seen = grads * weights[span].astype(F32)
            row_dot = row_dot + jnp.sum(seen, axis=0, keepdims=True)
        fin[0:1] = local[2:3]
        fin[1:2] = local[3:4]
        fin[2:3] = row_dot

    def attend_keys(q, scores, keys, fin, pg, gq, after_keys, before_queries=lambda: None):
        row_dot = fin[2:3]

        def grads_of_scores(i, carry):
            span = pl.ds(i * tile, tile)
            score_grads[span] = (scores[span] * (prob_grads[span] - row_dot)).astype(BF16)
            return carry

        per_chunk = chunk // tile
        for c in range(CHUNKS):
            lax.fori_loop(c * per_chunk, (c + 1) * per_chunk, grads_of_scores, 0)
            part = dot(score_grads[pl.ds(c * chunk, chunk)], q[...]) * scale
            pg[CHUNKS + c] = part.astype(BF16)
            after_keys(c)
        before_queries()
        gq_t = dot(keys[...].T, score_grads[...]) * scale
        for h in range(heads):
            gq[pl.ds(h * rows, rows)] = gq_t[:, h * rows : (h + 1) * rows].T.astype(BF16)

    def nothing(*args):
        pass

    def middle_part(c):
        return jnp.where(my_dest == r, own[c], edge_kv[c])

    def guest_part(c):
        return jnp.where(opp_dest == r, own[c], edge_kv[c])

    def edge_part(c):
        relay_send(c).wait_recv()
        return jnp.where(my_dest == r, own[c], relay_in[c])

    def pass_on(*chunks):
        for c in chunks:
            edge_send(c).wait_recv()
            pass_kv[c] = jnp.where(far_dest == r, own[c], edge_kv[c])
            pass_send(c).start()

    def pump(*chunks):
        for c in chunks:
            pass_send(c).wait_recv()
            relay_kv[c] = jnp.where(mate_dest == r, own[c], pass_in[c])
            relay_send(c).start()

    def forward(*chunks):
        for c in chunks:
            pg_edge_send(c).wait_recv()
            pg_far_send(c).start()

    @pl.when(is_middle)
    def _():
        pass_on(0, 1)
        attend_scores(q_rows, middle_part, (0, 1), scores, keys, local_own)

    hid_copy.wait()
    for copy in w_copies:
        copy.wait()
    for step in (1, 3):
        hid_from_y(step).wait_recv()
        hid_onward(step).start()
        hid_to_sibling(step).start()

    @pl.when(is_middle)
    def _():
        pump(0)
        pass_on(2, 3)
        for c in range(2, CHUNKS):
            query_send(c).start()
        attend_scores(q_rows, middle_part, (2, 3), scores, keys, local_own)
        pump(1)

    resp = dot(hid[0, 0], w[y_peer(0)])
    for step in (1, 3):
        resp = resp + dot(hid[step, 0], w[y_peer(step)])
    for slot in (0, 2):
        place = pl.ds(slot // 2 * half, half)
        along_t(
            hid.at[3 - slot, 0, place], hid.at[2, 0, place], hid_ys.at[slot], hid_yr.at[slot], sibling
        ).wait_recv()
    hid_to_sibling(2).start()

    @pl.when(is_middle)
    def _():
        pump(2)
        pass_on(4, 5)

    resp = resp + dot(hid[2, 0], w[y_peer(2)])
    for step in (0, 1, 3, 2):
        hid_to_sibling(step).wait_recv()
        resp = resp + dot(hid[step, 1], w[lax.rem(y + step, 4) * 2 + 1 - core])
    resp_kv[...] = resp.astype(BF16)

    @pl.when(is_middle)
    def _():
        pump(3)

    key_pos = lax.broadcasted_iota(jnp.int32, (rows, all_rows), 0)
    row_pos = lax.rem(lax.broadcasted_iota(jnp.int32, (rows, all_rows), 1), rows)
    visible = (key_pos <= row_pos) & (key_pos < length)
    resp_scores[...] = jnp.where(visible, dot_nt(resp_kv[:, :HD], q_rows[...]), -1e30)
    resp_prob_grads[...] = dot_nt(resp_kv[:, HD:], u_rows[...])
    resp_peak = jnp.max(resp_scores[...], axis=0, keepdims=True)
    resp_exp = jnp.exp2((resp_scores[...] - resp_peak) * factor)
    stat_resp[0:1] = resp_peak
    stat_resp[1:2] = jnp.sum(resp_exp, axis=0, keepdims=True)
    stat_resp[2:3] = jnp.sum(resp_exp * resp_prob_grads[...], axis=0, keepdims=True)

    def gh_to_sibling(step):
        return along_t(
            sib_send.at[step], sib_recv.at[step], gh_ss.at[step], gh_sr.at[step], sibling
        )

    def gh_to_y(step):
        return along_t(
            y_send.at[step], y_recv.at[4 - step], gh_ys.at[step], gh_yr.at[4 - step], y_peer(step)
        )

    def gh_from_y(step):
        return along_t(
            y_send.at[step], y_recv.at[step], gh_ys.at[step], gh_yr.at[step], y_peer(step)
        )

    def gh_half(step):
        place = pl.ds(0 if step == 1 else half, half)
        slot = 0 if step == 1 else 2
        return along_t(
            y_send.at[2, place], y_half.at[step // 2], gh_ys.at[slot], gh_yr.at[slot], y_peer(step)
        )

    def finish_resp():
        whole = jnp.where(in_half, fin_own[...], fin_back[...])
        probs = jnp.exp2((resp_scores[...] - whole[0:1]) * factor) * whole[1:2]
        grad_value = dot(probs.astype(BF16), u_rows[...]).astype(BF16)
        resp_score_grads[...] = (probs * (resp_prob_grads[...] - whole[2:3])).astype(BF16)
        grad_key = (dot(resp_score_grads[...], q_rows[...]) * scale).astype(BF16)
        resp_grads[...] = jnp.concatenate([grad_key, grad_value], axis=1)
        for step in (2, 1, 3, 0):
            shard = lax.rem(y + step, 4) * 2 + 1 - core
            sib_send[step] = dot_nt(resp_grads[...], w[shard]).astype(BF16)
            gh_to_sibling(step).start()

    def hidden_terms():
        for step in (2, 1, 3, 0):
            gh_to_sibling(step).wait_recv()
            term = dot_nt(resp_grads[...], w[y_peer(step)]) + sib_recv[step].astype(F32)
            y_send[step] = term.astype(BF16)
            if step == 2:
                gh_half(1).start()
                gh_half(3).start()

    def hidden_onward():
        for step in (1, 3):
            gh_half(step).wait_recv()
            place = pl.ds(0 if step == 1 else half, half)
            both = y_send[step, place].astype(F32) + y_half[step // 2].astype(F32)
            y_send[step, place] = both.astype(BF16)
            gh_to_y(step).start()

    def hidden_sum():
        summed = y_send[0].astype(F32)
        for step in (1, 3):
            gh_from_y(step).wait_recv()
            summed = summed + y_recv[step].astype(F32)
        gh_out[...] = summed.astype(BF16)

    def query_sum(c):
        @pl.when(is_middle)
        def _():
            result_send(c).wait_recv()

        for h in range(c * heads // CHUNKS, (c + 1) * heads // CHUNKS):
            place = pl.ds(h * rows, rows)
            prompt_part = jnp.where(in_half, gq_own[place], gq_back[place]).astype(F32)
            gq = prompt_part + resp_queries[place]
            gq_out[:, pl.ds(h * HD, HD)] = gq.astype(BF16)

    def kept(flag, value):
        return jnp.where(flag, value.astype(F32), 0.0)

    def collect(c):
        @pl.when(is_middle)
        def _():
            pg_far_send(c).wait_recv()
            passed = kept(my_dest == mate, pg_own[c]) + kept(opp_dest == mate, pg_guest[c])
            pg_relay[c] = (passed + kept(far_dest == mate, pg_far[c])).astype(BF16)
            pg_back_send(c).start()

        @pl.when(is_edge)
        def _():
            pg_back_send(c).wait_recv()

        summed = kept(my_dest == r, pg_own[c]) + kept(is_edge, pg_back[c])
        summed = summed + kept(is_middle & (opp_dest == r), pg_guest[c])
        summed = summed + kept(is_middle & (mate_dest == r), pg_edge[c])
        summed = summed + kept(is_middle & (far_dest == r), pg_far[c])
        gp_out[1 - c // CHUNKS, pl.ds((c % CHUNKS) * chunk, chunk)] = summed.astype(BF16)

    @pl.when(is_middle)
    def _():
        stat_send().start()
        pass_on(6, 7)
        for c in range(CHUNKS, total):
            query_send(c).start()
        attend_exponents(scores, local_own)
        for c in range(CHUNKS):
            query_send(c).wait_recv()
        attend_scores(guest_q, guest_part, range(CHUNKS), guest_scores, guest_keys, local_guest)
        pump(4)
        attend_exponents(guest_scores, local_guest)
        attend_values(u_rows, scores, local_own, stat_resp, pg_own, nothing, lambda: pump(5))
        pump(6)
        attend_dot(u_rows, lambda c: middle_part(CHUNKS + c), local_own, fin_own)
        pump(7)
        attend_keys(q_rows, scores, keys, fin_own, pg_own, gq_own, nothing)
        forward(0, 1, 2, 3)
        for c in range(total):
            pass_send(c).wait_send()
            relay_send(c).wait_send()
        stat_send().wait()
        for c in range(CHUNKS, total):
            query_send(c).wait_recv()
        attend_values(guest_u, guest_scores, local_guest, stat_guest, pg_guest, nothing, nothing)
        attend_dot(guest_u, lambda c: guest_part(CHUNKS + c), local_guest, fin_guest)
        fin_send().start()
        attend_keys(
            guest_q, guest_scores, guest_keys, fin_guest, pg_guest, gq_guest,
            lambda c: (forward(CHUNKS + c), collect(c)),
        )
        for c in range(CHUNKS):
            result_send(c).start()
        fin_send().wait()
        finish_resp()
        for c in range(total):
            query_send(c).wait_send()

    @pl.when(is_edge)
    def _():
        attend_scores(q_rows, edge_part, range(CHUNKS), scores, keys, local_own)
        attend_exponents(scores, local_own)
        attend_values(
            u_rows, scores, local_own, stat_resp, pg_own, lambda c: pg_edge_send(c).start(), nothing
        )
        for c in range(total):
            edge_send(c).wait_send()
        attend_dot(u_rows, lambda c: edge_part(CHUNKS + c), local_own, fin_own)
        attend_keys(
            q_rows, scores, keys, fin_own, pg_own, gq_own, lambda c: pg_edge_send(CHUNKS + c).start(),
            finish_resp,
        )

    for step in range(4):
        hid_to_sibling(step).wait_send()
        if step in (1, 3):
            hid_to_y(step).wait_send()
            hid_onward(step).wait_send()

    hidden_terms()

    def resp_query_terms():
        gq_t = dot(resp_kv[:, :HD].T, resp_score_grads[...]) * scale
        for h in range(heads):
            resp_queries[pl.ds(h * rows, rows)] = gq_t[:, h * rows : (h + 1) * rows].T

    @pl.when(is_middle)
    def _():
        collect(4)
        collect(5)
        hidden_onward()
        collect(6)
        resp_query_terms()
        collect(7)
        for c in range(CHUNKS - 1):
            query_sum(c)
        hidden_sum()
        query_sum(CHUNKS - 1)

    @pl.when(is_edge)
    def _():
        resp_query_terms()
        hidden_onward()
        for c in range(CHUNKS):
            query_sum(c)
        for c in range(CHUNKS):
            collect(c)
        hidden_sum()
        for c in range(CHUNKS, total):
            collect(c)

    for step in range(4):
        gh_to_sibling(step).wait_send()
        if step in (1, 3):
            gh_half(step).wait_send()
            gh_to_y(step).wait_send()

    @pl.when(is_edge)
    def _():
        for c in range(total):
            pg_edge_send(c).wait_send()

    @pl.when(is_middle)
    def _():
        for c in range(CHUNKS):
            result_send(c).wait_send()
        for c in range(total):
            pg_far_send(c).wait_send()
            pg_back_send(c).wait_send()


def write_kernel(a_ref, b_ref, c_ref, a_out, b_out, c_out, sems):
    copies = [
        pltpu.make_async_copy(src, dst, sems.at[i])
        for i, (src, dst) in enumerate(((c_ref, c_out), (a_ref, a_out), (b_ref, b_out)))
    ]
    for copy in copies:
        copy.start()
    for copy in copies:
        copy.wait()


def write_out(*arrays):
    anywhere = pl.BlockSpec(memory_space=pl.ANY)
    return pl.pallas_call(
        write_kernel,
        out_shape=tuple(jax.ShapeDtypeStruct(a.shape, a.dtype) for a in arrays),
        in_specs=[anywhere] * 3,
        out_specs=[anywhere] * 3,
        scratch_shapes=[pltpu.SemaphoreType.DMA((3,))],
        compiler_params=pltpu.CompilerParams(vmem_limit_bytes=1024 * 1024),
        name="write_out",
    )(*arrays)


def local(hidden, queries, out_grad, w_key, w_value, prompt_kv, block_dest, resp_len):
    rows, q_cols = queries.shape
    shard_cols = hidden.shape[1]
    shards = w_key.shape[0] // shard_cols
    kv_cols = w_key.shape[1]
    prompt_len = prompt_kv.shape[2]
    chunk = prompt_len // CHUNKS
    total = 2 * CHUNKS
    all_rows = q_cols // HD * rows
    heads = q_cols // HD
    dma = pltpu.SemaphoreType.DMA
    part = pltpu.VMEM((total, chunk, kv_cols), BF16)
    shard = (rows, shard_cols)
    hbm = pl.BlockSpec(memory_space=pltpu.HBM)
    rows_of_heads = pltpu.VMEM((all_rows, HD), BF16)
    stat = pltpu.VMEM((8, all_rows), F32)
    scratch = (
        [part] * 12
        + [rows_of_heads] * 7
        + [
            pltpu.VMEM((prompt_len, HD), BF16),
            pltpu.VMEM((prompt_len, HD), BF16),
            pltpu.VMEM((prompt_len, all_rows), F32),
            pltpu.VMEM((prompt_len, all_rows), F32),
            pltpu.VMEM((prompt_len, all_rows), F32),
            pltpu.VMEM((prompt_len, all_rows), BF16),
            pltpu.VMEM((prompt_len, all_rows), BF16),
            pltpu.VMEM((rows, 2 * HD), BF16),
            pltpu.VMEM((all_rows, HD), F32),
            pltpu.VMEM((rows, all_rows), F32),
            pltpu.VMEM((rows, all_rows), F32),
            pltpu.VMEM((rows, all_rows), BF16),
            pltpu.VMEM((rows, 2 * HD), BF16),
        ]
        + [stat] * 7
        + [
            pltpu.VMEM((shards, shard_cols, 2 * kv_cols), BF16),
            pltpu.VMEM((4, 2) + shard, BF16),
        ]
        + [pltpu.VMEM((4,) + shard, BF16)] * 4
        + [pltpu.VMEM((2, rows // 2, shard_cols), BF16)]
        + [dma((total,))] * 14
        + [dma((CHUNKS,))] * 2
        + [dma((2,))] * 2
        + [dma((4,))] * 8
        + [dma((total,)), dma((2 * heads,)), dma((2,)), dma]
        + [pltpu.SMEM(block_dest.shape, jnp.int32), pltpu.SMEM(resp_len.shape, jnp.int32), dma((2,))]
    )
    grad_query, grad_hidden, grad_prompt = pl.pallas_call(
        kernel,
        out_shape=(
            pltpu.VMEM(queries.shape, BF16),
            pltpu.VMEM(hidden.shape, BF16),
            pltpu.VMEM(prompt_kv.shape[1:], BF16),
        ),
        in_specs=[hbm] * 8,
        out_specs=[pl.BlockSpec(memory_space=pltpu.VMEM)] * 3,
        scratch_shapes=scratch,
        compiler_params=pltpu.CompilerParams(
            collective_id=0, has_side_effects=True, vmem_limit_bytes=60 * 1024 * 1024
        ),
        name="attention_backward",
    )(
        block_dest, resp_len, hidden, queries, out_grad,
        w_key.reshape(shards, shard_cols, kv_cols), w_value.reshape(shards, shard_cols, kv_cols),
        prompt_kv[0],
    )
    return write_out(grad_query, grad_hidden, grad_prompt[None])


def solution(mesh):
    return jax.shard_map(
        local,
        mesh=mesh,
        in_specs=(
            P("dp", "tensor"),
            P("dp", "tensor"),
            P("dp", "tensor"),
            P(None, "tensor"),
            P(None, "tensor"),
            P("dp", None, None, "tensor"),
            P(),
            P(),
        ),
        out_specs=(P("dp", "tensor"), P("dp", "tensor"), P("dp", None, None, "tensor")),
        check_vma=False,
    )
```

time: 59.6 us -> 56.3 us (0.945)
  Pallas kernels: 58.9 us -> 55.4 us
    pallas_call x1, Pallas kernels: 57.9 us -> 54.4 us  [local(): pl.pallas_call(kernel, out_shape=(pltpu.VMEM(queries.shape, BF16), pltpu....]
where the time goes in v4:
time: 56.3 us; the launch traced here: 56.2 us
  Pallas kernels  55.4 us (98%)
  between operations  0.8 us (1%)
    pallas_call x1, Pallas kernels, local(): pl.pallas_call(kernel, out_shape=(pltpu.VMEM(queries.shape, BF16), pltpu....  54.4 us

profile of v4, /device:TPU:1, one launch (start us, length us, event | category | flops | bytes accessed | tf_op | source)
XLA Modules:
  0.0 56.2 jit_solution(11562796241086937984)
XLA Ops:
  0.6 54.4 %attention_backward.1 = (bf16[128,1024]{1,0:T(8,128)(2,1)S(1)}, bf16[128,640]{1,0:T(8,128)(2,1)S(1)}, bf16[2,1024,128]{2,1,0:T(8,128)(2,1)S(1)}) custom-call(s32[64]{0:T(128)} %dest_ref.1, s32[64]{0:T(128)} %len_ref.1, bf16[128,640]{1,0:T(8,128)(2,1)} %hidden_ref.1, bf16[128,1024]{1,0:T(8,128)(2,1)} %q_ref.1, bf16[128,1024]{1,0:T(8,128)(2,1)} %u_ref.1, ...), custom_call_target="tpu_custom_call" | custom-call | tf_op jit(solution)/shard_map/attention_backward/pallas_call | solution.py:651
  55.1 1.0 %write_out.1 = (bf16[128,1024]{1,0:T(8,128)(2,1)}, bf16[128,640]{1,0:T(8,128)(2,1)}, bf16[1,2,1024,128]{3,2,1,0:T(8,128)(2,1)}) custom-call(bf16[128,1024]{1,0:T(8,128)(2,1)S(1)} %get-tuple-element.6.a_ref, bf16[128,640]{1,0:T(8,128)(2,1)S(1)} %get-tuple-element.7.b_ref, bf16[1,2,1024,128]{3,2,1,0:T(8,128)(2,1)S(1)} %bitcast.4), custom_call_target="tpu_custom_call" | custom-call | tf_op jit(solution)/shard_map/write_out/pallas_call | solution.py:592

commit v5 on v4

--- a/solution.py
+++ b/solution.py
@@ -79,13 +79,14 @@
     def own_copy(c):
         return pltpu.make_async_copy(kv_part(c), own.at[c], own_sem.at[c])
 
-    def head_copies(h):
+    def q_copy(h):
+        span = pl.ds(h * HD, HD)
+        return pltpu.make_async_copy(q_ref.at[:, span], q_rows.at[pl.ds(h * rows, rows)], qu_sem.at[h])
+
+    def u_copy(h):
         span = pl.ds(h * HD, HD)
         place = pl.ds(h * rows, rows)
-        return (
-            pltpu.make_async_copy(q_ref.at[:, span], q_rows.at[place], qu_sem.at[h]),
-            pltpu.make_async_copy(u_ref.at[:, span], u_rows.at[place], qu_sem.at[heads + h]),
-        )
+        return pltpu.make_async_copy(u_ref.at[:, span], u_rows.at[place], qu_sem.at[heads + h])
 
     w_copies = (
         pltpu.make_async_copy(wk_ref, w.at[:, :, pl.ds(0, HD)], w_sem.at[0]),
@@ -95,17 +96,6 @@
     dest_copy = pltpu.make_async_copy(dest_ref, dests, small_sem.at[0])
     len_copy = pltpu.make_async_copy(len_ref, lengths, small_sem.at[1])
 
-    dest_copy.start()
-    len_copy.start()
-    for h in range(heads):
-        for copy in head_copies(h):
-            copy.start()
-    for c in range(total):
-        own_copy(c).start()
-    hid_copy.start()
-    for copy in w_copies:
-        copy.start()
-
     barrier = pltpu.get_barrier_semaphore()
     for step in range(1, GROUP):
         pl.semaphore_signal(
@@ -115,6 +105,92 @@
             barrier, inc=1, device_id={"tensor": y_peer(step)}, device_id_type=MESH
         )
     pl.semaphore_signal(barrier, inc=1, device_id={"tensor": sibling}, device_id_type=MESH)
+
+    for h in range(heads):
+        q_copy(h).start()
+    dest_copy.start()
+    len_copy.start()
+    for h in range(heads):
+        u_copy(h).start()
+    hid_copy.start()
+    for c in range(total):
+        own_copy(c).start()
+    for copy in w_copies:
+        copy.start()
+    for h in range(heads):
+        q_copy(h).wait()
+    pl.semaphore_wait(barrier, 2 * (GROUP - 1) + 1)
+
+    def edge_send(c):
+        return along_z(kv_part(c), edge_kv.at[c], kv_s.at[c], kv_r.at[c], mate)
+
+    def row_part(c):
+        return pl.ds(c * (all_rows // CHUNKS), all_rows // CHUNKS)
+
+    def query_send(c):
+        src, dst = (q_rows, guest_q) if c < CHUNKS else (u_rows, guest_u)
+        place = row_part(c % CHUNKS)
+        return along_z(src.at[place], dst.at[place], q_s.at[c], q_r.at[c], opp)
+
+    def pass_send(c):
+        return along_z(pass_kv.at[c], pass_in.at[c], pass_s.at[c], pass_r.at[c], opp)
+
+    def relay_send(c):
+        return along_z(relay_kv.at[c], relay_in.at[c], relay_s.at[c], relay_r.at[c], mate)
+
+    def stat_send():
+        return along_z(stat_resp, stat_guest, stat_s.at[0], stat_r.at[0], opp)
+
+    def fin_send():
+        return along_z(fin_guest, fin_back, stat_s.at[1], stat_r.at[1], opp)
+
+    def result_send(c):
+        place = row_part(c)
+        return along_z(gq_guest.at[place], gq_back.at[place], res_s.at[c], res_r.at[c], opp)
+
+    def pg_edge_send(c):
+        return along_z(pg_own.at[c], pg_edge.at[c], pe_s.at[c], pe_r.at[c], mate)
+
+    def pg_far_send(c):
+        return along_z(pg_edge.at[c], pg_far.at[c], far_s.at[c], far_r.at[c], opp)
+
+    def pg_back_send(c):
+        return along_z(pg_relay.at[c], pg_back.at[c], back_s.at[c], back_r.at[c], mate)
+
+    @pl.when(is_edge)
+    def _():
+        for c in range(total):
+            edge_send(c).start()
+
+    @pl.when(is_middle)
+    def _():
+        for c in range(2):
+            query_send(c).start()
+
+    half = rows // 2
+
+    def hid_to_y(step):
+        return along_t(
+            hidden_ref, hid.at[4 - step, 0], hid_ys.at[step], hid_yr.at[4 - step], y_peer(step)
+        )
+
+    def hid_from_y(step):
+        return along_t(hidden_ref, hid.at[step, 0], hid_ys.at[step], hid_yr.at[step], y_peer(step))
+
+    def hid_onward(step):
+        place = pl.ds(0 if step == 3 else half, half)
+        slot = 0 if step == 3 else 2
+        return along_t(
+            hid.at[step, 0, place], hid.at[2, 0, place], hid_ys.at[slot], hid_yr.at[slot], y_peer(4 - step)
+        )
+
+    def hid_to_sibling(step):
+        src = hidden_ref if step == 0 else hid.at[step, 0]
+        return along_t(src, hid.at[step, 1], hid_ss.at[step], hid_sr.at[step], sibling)
+
+    for step in (1, 3):
+        hid_to_y(step).start()
+    hid_to_sibling(0).start()
 
     dest_copy.wait()
     len_copy.wait()
@@ -126,8 +202,7 @@
     in_half = is_edge | (my_dest == r) | (my_dest == mate)
 
     for h in range(heads):
-        for copy in head_copies(h):
-            copy.wait()
+        u_copy(h).wait()
 
     def mask_upstream(h, carry):
         place = pl.ds(h * rows, rows)
@@ -136,81 +211,8 @@
         return carry
 
     lax.fori_loop(0, heads, mask_upstream, 0)
-    pl.semaphore_wait(barrier, 2 * (GROUP - 1) + 1)
-
-    def edge_send(c):
-        return along_z(own.at[c], edge_kv.at[c], kv_s.at[c], kv_r.at[c], mate)
-
-    def row_part(c):
-        return pl.ds(c * (all_rows // CHUNKS), all_rows // CHUNKS)
-
-    def query_send(c):
-        src, dst = (q_rows, guest_q) if c < CHUNKS else (u_rows, guest_u)
-        place = row_part(c % CHUNKS)
-        return along_z(src.at[place], dst.at[place], q_s.at[c], q_r.at[c], opp)
-
-    def pass_send(c):
-        return along_z(pass_kv.at[c], pass_in.at[c], pass_s.at[c], pass_r.at[c], opp)
-
-    def relay_send(c):
-        return along_z(relay_kv.at[c], relay_in.at[c], relay_s.at[c], relay_r.at[c], mate)
-
-    def stat_send():
-        return along_z(stat_resp, stat_guest, stat_s.at[0], stat_r.at[0], opp)
-
-    def fin_send():
-        return along_z(fin_guest, fin_back, stat_s.at[1], stat_r.at[1], opp)
-
-    def result_send(c):
-        place = row_part(c)
-        return along_z(gq_guest.at[place], gq_back.at[place], res_s.at[c], res_r.at[c], opp)
-
-    def pg_edge_send(c):
-        return along_z(pg_own.at[c], pg_edge.at[c], pe_s.at[c], pe_r.at[c], mate)
-
-    def pg_far_send(c):
-        return along_z(pg_edge.at[c], pg_far.at[c], far_s.at[c], far_r.at[c], opp)
-
-    def pg_back_send(c):
-        return along_z(pg_relay.at[c], pg_back.at[c], back_s.at[c], back_r.at[c], mate)
-
-    @pl.when(is_edge)
-    def _():
-        for c in range(total):
-            own_copy(c).wait()
-            edge_send(c).start()
-
-    @pl.when(is_middle)
-    def _():
-        for c in range(2):
-            query_send(c).start()
-        for c in range(total):
-            own_copy(c).wait()
-
-    half = rows // 2
-
-    def hid_to_y(step):
-        return along_t(
-            hidden_ref, hid.at[4 - step, 0], hid_ys.at[step], hid_yr.at[4 - step], y_peer(step)
-        )
-
-    def hid_from_y(step):
-        return along_t(hidden_ref, hid.at[step, 0], hid_ys.at[step], hid_yr.at[step], y_peer(step))
-
-    def hid_onward(step):
-        place = pl.ds(0 if step == 3 else half, half)
-        slot = 0 if step == 3 else 2
-        return along_t(
-            hid.at[step, 0, place], hid.at[2, 0, place], hid_ys.at[slot], hid_yr.at[slot], y_peer(4 - step)
-        )
-
-    def hid_to_sibling(step):
-        src = hidden_ref if step == 0 else hid.at[step, 0]
-        return along_t(src, hid.at[step, 1], hid_ss.at[step], hid_sr.at[step], sibling)
-
-    for step in (1, 3):
-        hid_to_y(step).start()
-    hid_to_sibling(0).start()
+    for c in range(total):
+        own_copy(c).wait()
 
     def attend_scores(q, key_part, chunks, scores, keys, local):
         for c in chunks:
@@ -233,7 +235,7 @@
         sums = lax.fori_loop(0, prompt_len // tile, exponents, jnp.zeros((8, all_rows), F32))
         local[1:2] = jnp.sum(sums, axis=0, keepdims=True)
 
-    def attend_values(u, scores, local, stats, pg, after_values, between):
+    def attend_share(scores, local, stats):
         peak = jnp.maximum(local[0:1], stats[0:1])
         fade = jnp.exp2((local[0:1] - peak) * factor)
         resp_fade = jnp.exp2((stats[0:1] - peak) * factor)
@@ -248,10 +250,11 @@
             return carry
 
         lax.fori_loop(0, prompt_len // tile, normalise, 0)
-        between()
         local[2:3] = peak
         local[3:4] = inverse
         local[4:5] = stats[2:3] * resp_fade * inverse
+
+    def attend_values(u, pg, after_values):
         for c in range(CHUNKS):
             pg[c] = dot(weights[pl.ds(c * chunk, chunk)], u[...]).astype(BF16)
             after_values(c)
@@ -477,39 +480,49 @@
         attend_scores(guest_q, guest_part, range(CHUNKS), guest_scores, guest_keys, local_guest)
         pump(4)
         attend_exponents(guest_scores, local_guest)
-        attend_values(u_rows, scores, local_own, stat_resp, pg_own, nothing, lambda: pump(5))
+        attend_share(scores, local_own, stat_resp)
+        pump(5)
+        attend_values(u_rows, pg_own, nothing)
         pump(6)
         attend_dot(u_rows, lambda c: middle_part(CHUNKS + c), local_own, fin_own)
         pump(7)
         attend_keys(q_rows, scores, keys, fin_own, pg_own, gq_own, nothing)
-        forward(0, 1, 2, 3)
+        forward(0, 1)
+        stat_send().wait()
+        attend_share(guest_scores, local_guest, stat_guest)
         for c in range(total):
             pass_send(c).wait_send()
             relay_send(c).wait_send()
-        stat_send().wait()
         for c in range(CHUNKS, total):
             query_send(c).wait_recv()
-        attend_values(guest_u, guest_scores, local_guest, stat_guest, pg_guest, nothing, nothing)
         attend_dot(guest_u, lambda c: guest_part(CHUNKS + c), local_guest, fin_guest)
         fin_send().start()
+        forward(2, 3)
+        attend_values(guest_u, pg_guest, nothing)
+        collect(0)
+        collect(1)
+        forward(4)
+        fin_send().wait()
+        forward(5)
+        finish_resp()
+        forward(6, 7)
+        collect(2)
+        collect(3)
+        hidden_terms()
         attend_keys(
             guest_q, guest_scores, guest_keys, fin_guest, pg_guest, gq_guest,
-            lambda c: (forward(CHUNKS + c), collect(c)),
+            lambda c: collect(CHUNKS + c) if c < 2 else None,
         )
         for c in range(CHUNKS):
             result_send(c).start()
-        fin_send().wait()
-        finish_resp()
-        for c in range(total):
-            query_send(c).wait_send()
+        hidden_onward()
 
     @pl.when(is_edge)
     def _():
         attend_scores(q_rows, edge_part, range(CHUNKS), scores, keys, local_own)
         attend_exponents(scores, local_own)
-        attend_values(
-            u_rows, scores, local_own, stat_resp, pg_own, lambda c: pg_edge_send(c).start(), nothing
-        )
+        attend_share(scores, local_own, stat_resp)
+        attend_values(u_rows, pg_own, lambda c: pg_edge_send(c).start())
         for c in range(total):
             edge_send(c).wait_send()
         attend_dot(u_rows, lambda c: edge_part(CHUNKS + c), local_own, fin_own)
@@ -524,8 +537,6 @@
             hid_to_y(step).wait_send()
             hid_onward(step).wait_send()
 
-    hidden_terms()
-
     def resp_query_terms():
         gq_t = dot(resp_kv[:, :HD].T, resp_score_grads[...]) * scale
         for h in range(heads):
@@ -533,23 +544,29 @@
 
     @pl.when(is_middle)
     def _():
-        collect(4)
-        collect(5)
-        hidden_onward()
         collect(6)
+        collect(7)
         resp_query_terms()
-        collect(7)
+        for c in range(total):
+            query_send(c).wait_send()
         for c in range(CHUNKS - 1):
             query_sum(c)
+        for c in range(total):
+            pg_far_send(c).wait_send()
         hidden_sum()
+        for c in range(total - 2):
+            pg_back_send(c).wait_send()
         query_sum(CHUNKS - 1)
 
     @pl.when(is_edge)
     def _():
+        hidden_terms()
         resp_query_terms()
         hidden_onward()
         for c in range(CHUNKS):
             query_sum(c)
+        for c in range(total):
+            pg_edge_send(c).wait_send()
         for c in range(CHUNKS):
             collect(c)
         hidden_sum()
@@ -562,17 +579,11 @@
             gh_half(step).wait_send()
             gh_to_y(step).wait_send()
 
-    @pl.when(is_edge)
-    def _():
-        for c in range(total):
-            pg_edge_send(c).wait_send()
-
     @pl.when(is_middle)
     def _():
         for c in range(CHUNKS):
             result_send(c).wait_send()
-        for c in range(total):
-            pg_far_send(c).wait_send()
+        for c in range(total - 2, total):
             pg_back_send(c).wait_send()
 
 

time: 56.3 us -> 54.2 us (0.963)
  Pallas kernels: 55.4 us -> 52.7 us
    pallas_call x1, Pallas kernels: 54.4 us -> 51.8 us  [local(): pl.pallas_call(kernel, out_shape=(pltpu.VMEM(queries.shape, BF16), pltpu....]
where the time goes in v5:
time: 54.2 us; the launch traced here: 53.5 us
  Pallas kernels  52.7 us (97%)
  between operations  0.8 us (1%)
    pallas_call x1, Pallas kernels, local(): pl.pallas_call(kernel, out_shape=(pltpu.VMEM(queries.shape, BF16), pltpu....  51.8 us

profile of v5, /device:TPU:1, one launch (start us, length us, event | category | flops | bytes accessed | tf_op | source)
XLA Modules:
  0.0 53.5 jit_solution(7576505260500327285)
XLA Ops:
  0.6 51.8 %attention_backward.1 = (bf16[128,1024]{1,0:T(8,128)(2,1)S(1)}, bf16[128,640]{1,0:T(8,128)(2,1)S(1)}, bf16[2,1024,128]{2,1,0:T(8,128)(2,1)S(1)}) custom-call(s32[64]{0:T(128)} %dest_ref.1, s32[64]{0:T(128)} %len_ref.1, bf16[128,640]{1,0:T(8,128)(2,1)} %hidden_ref.1, bf16[128,1024]{1,0:T(8,128)(2,1)} %q_ref.1, bf16[128,1024]{1,0:T(8,128)(2,1)} %u_ref.1, ...), custom_call_target="tpu_custom_call" | custom-call | tf_op jit(solution)/shard_map/attention_backward/pallas_call | solution.py:662
  52.4 1.0 %write_out.1 = (bf16[128,1024]{1,0:T(8,128)(2,1)}, bf16[128,640]{1,0:T(8,128)(2,1)}, bf16[1,2,1024,128]{3,2,1,0:T(8,128)(2,1)}) custom-call(bf16[128,1024]{1,0:T(8,128)(2,1)S(1)} %get-tuple-element.6.a_ref, bf16[128,640]{1,0:T(8,128)(2,1)S(1)} %get-tuple-element.7.b_ref, bf16[1,2,1024,128]{3,2,1,0:T(8,128)(2,1)S(1)} %bitcast.4), custom_call_target="tpu_custom_call" | custom-call | tf_op jit(solution)/shard_map/write_out/pallas_call | solution.py:603

commit v6 on v5

--- a/solution.py
+++ b/solution.py
@@ -164,7 +164,7 @@
 
     @pl.when(is_middle)
     def _():
-        for c in range(2):
+        for c in range(3):
             query_send(c).start()
 
     half = rows // 2
@@ -259,17 +259,20 @@
             pg[c] = dot(weights[pl.ds(c * chunk, chunk)], u[...]).astype(BF16)
             after_values(c)
 
-    def attend_dot(u, value_part, local, fin):
-        row_dot = local[4:5]
-        for c in range(CHUNKS):
-            span = pl.ds(c * chunk, chunk)
-            grads = dot_nt(value_part(c), u[...])
-            prob_grads[span] = grads
-            seen = grads * weights[span].astype(F32)
-            row_dot = row_dot + jnp.sum(seen, axis=0, keepdims=True)
+    def attend_dot(u, value_part, local, fin, parts=1, before=lambda part: None):
+        for part in range(parts):
+            before(part)
+            place = pl.ds(part * (all_rows // parts), all_rows // parts)
+            row_dot = local[4:5, place]
+            for c in range(CHUNKS):
+                span = pl.ds(c * chunk, chunk)
+                grads = dot_nt(value_part(c), u[place])
+                prob_grads[span, place] = grads
+                seen = grads * weights[span, place].astype(F32)
+                row_dot = row_dot + jnp.sum(seen, axis=0, keepdims=True)
+            fin[2:3, place] = row_dot
         fin[0:1] = local[2:3]
         fin[1:2] = local[3:4]
-        fin[2:3] = row_dot
 
     def attend_keys(q, scores, keys, fin, pg, gq, after_keys, before_queries=lambda: None):
         row_dot = fin[2:3]
@@ -337,8 +340,7 @@
     def _():
         pump(0)
         pass_on(2, 3)
-        for c in range(2, CHUNKS):
-            query_send(c).start()
+        query_send(3).start()
         attend_scores(q_rows, middle_part, (2, 3), scores, keys, local_own)
         pump(1)
 
@@ -493,9 +495,10 @@
         for c in range(total):
             pass_send(c).wait_send()
             relay_send(c).wait_send()
-        for c in range(CHUNKS, total):
-            query_send(c).wait_recv()
-        attend_dot(guest_u, lambda c: guest_part(CHUNKS + c), local_guest, fin_guest)
+        attend_dot(
+            guest_u, lambda c: guest_part(CHUNKS + c), local_guest, fin_guest,
+            CHUNKS, lambda part: query_send(CHUNKS + part).wait_recv(),
+        )
         fin_send().start()
         forward(2, 3)
         attend_values(guest_u, pg_guest, nothing)

time: 54.2 us -> 52.3 us (0.965)
  Pallas kernels: 52.7 us -> 51.2 us
    pallas_call x1, Pallas kernels: 51.8 us -> 50.3 us  [local(): pl.pallas_call(kernel, out_shape=(pltpu.VMEM(queries.shape, BF16), pltpu....]
where the time goes in v6:
time: 52.3 us; the launch traced here: 52 us
  Pallas kernels  51.2 us (98%)
  between operations  0.8 us (2%)
    pallas_call x1, Pallas kernels, local(): pl.pallas_call(kernel, out_shape=(pltpu.VMEM(queries.shape, BF16), pltpu....  50.3 us

profile of v6, /device:TPU:1, one launch (start us, length us, event | category | flops | bytes accessed | tf_op | source)
XLA Modules:
  0.0 52.0 jit_solution(15216961305207125256)
XLA Ops:
  0.6 50.3 %attention_backward.1 = (bf16[128,1024]{1,0:T(8,128)(2,1)S(1)}, bf16[128,640]{1,0:T(8,128)(2,1)S(1)}, bf16[2,1024,128]{2,1,0:T(8,128)(2,1)S(1)}) custom-call(s32[64]{0:T(128)} %dest_ref.1, s32[64]{0:T(128)} %len_ref.1, bf16[128,640]{1,0:T(8,128)(2,1)} %hidden_ref.1, bf16[128,1024]{1,0:T(8,128)(2,1)} %q_ref.1, bf16[128,1024]{1,0:T(8,128)(2,1)} %u_ref.1, ...), custom_call_target="tpu_custom_call" | custom-call | tf_op jit(solution)/shard_map/attention_backward/pallas_call | solution.py:665
  50.9 1.0 %write_out.1 = (bf16[128,1024]{1,0:T(8,128)(2,1)}, bf16[128,640]{1,0:T(8,128)(2,1)}, bf16[1,2,1024,128]{3,2,1,0:T(8,128)(2,1)}) custom-call(bf16[128,1024]{1,0:T(8,128)(2,1)S(1)} %get-tuple-element.6.a_ref, bf16[128,640]{1,0:T(8,128)(2,1)S(1)} %get-tuple-element.7.b_ref, bf16[1,2,1024,128]{3,2,1,0:T(8,128)(2,1)S(1)} %bitcast.4), custom_call_target="tpu_custom_call" | custom-call | tf_op jit(solution)/shard_map/write_out/pallas_call | solution.py:606
